TPU v7x, 32 devices: a whole 2x2x4 slice. The times are simulated.
32 devices in a mesh: blk: 8 (over y, x, core), ax: 4 (over z).
Axes of the slice: x: 2, y: 2, z: 4, core: 2. Of those that a mesh axis runs over, the one named last changes fastest.
Arguments:
- adjoint: bfloat16 [5, 8, 256, 64, 128], P(None, 'blk', 'ax'), may hold values from -6 to 6
- density: bfloat16 [8, 256, 64, 128], P('blk', 'ax'), may hold values from 0.5 to 1.5
- velocity: bfloat16 [3, 8, 256, 64, 128], P(None, 'blk', 'ax'), may hold values from -3 to 3
- pressure: bfloat16 [8, 256, 64, 128], P('blk', 'ax'), may hold values from 0.5 to 1.5
- metrics: bfloat16 [9, 8, 256, 64, 128], P(None, 'blk', 'ax'), may hold values from -6 to 6
- links: int32 [3, 8, 48], replicated, may hold values from -1 to 47, as said below
Outputs:
- rhs: bfloat16 [5, 8, 256, 64, 128], P(None, 'blk', 'ax')
Inputs may be any that keep to these rules, and one draw needn't show every extreme that they name: links[0] is a source block or -1 (a physical boundary), links[1] a patch of that block, links[2] an orientation 0 or 1. No source patch is named twice. A block names at most 6 patches of any one source block, and some pair of blocks reaches exactly 6. The number of live patches differs between blocks, and at least one block has all 48 live.
All inputs are finite; a program needn't handle non-finite values.
Results may differ from a plain program's by a relative error of at most 0.001.
Values may be sent and summed in bfloat16 or wider, within the bound.
A program may use at most 256 MiB of HBM per device.

v0:
```python
import jax
import jax.numpy as jnp
from jax import lax
from jax.sharding import PartitionSpec as P

PW = 8


lhs_alpha = 1.0 / 3.0
near_coef = 7.0 / 9.0
far_coef = 1.0 / 36.0
heat_ratio = 1.4
penalty_weight = 1.0


def extended(cells, sides, width):
    for axis, dim in sides:
        count = lax.axis_size(axis)
        ends = count - 1
        head = lax.slice_in_dim(cells, 0, width, axis=dim)
        tail = lax.slice_in_dim(cells, cells.shape[dim] - width, cells.shape[dim], axis=dim)
        cells = jnp.concatenate(
            [
                lax.ppermute(tail, axis, [(i, (i + 1) % count) for i in range(ends)]),
                cells,
                lax.ppermute(head, axis, [((i + 1) % count, i) for i in range(ends)]),
            ],
            axis=dim,
        )
    return cells


def shortened(shard):

    def short(part):
        return part.astype(jnp.bfloat16) if part.dtype == jnp.float32 else part

    return jax.tree.map(short, shard)


def line_tables(line_cells):
    position = jnp.arange(line_cells, dtype=jnp.int32)
    middle = jnp.ones((line_cells,), jnp.float32)
    sub_diag = jnp.where(position > 0, lhs_alpha, 0.0).astype(jnp.float32)
    super_diag = jnp.where(position < line_cells - 1, lhs_alpha, 0.0).astype(jnp.float32)
    offset = position[None, :] - position[:, None]
    stencil = near_coef * ((offset == 1).astype(jnp.float32) - (offset == -1).astype(jnp.float32))
    stencil = stencil + far_coef * (
        (offset == 2).astype(jnp.float32) - (offset == -2).astype(jnp.float32)
    )
    inverse = lax.linalg.tridiagonal_solve(
        sub_diag, middle, super_diag, jnp.eye(line_cells, dtype=jnp.float32)
    )
    derivative = lax.linalg.tridiagonal_solve(sub_diag, middle, super_diag, stencil)
    return (inverse, derivative)


def widen(values):
    return values.astype(jnp.float32)


def flux_parts(gradient, metric, density_f, velocity, pressure_f):
    metric_a = widen(metric[0])
    metric_b = widen(metric[1])
    metric_c = widen(metric[2])
    contravariant = (
        metric_a * widen(velocity[0])
        + metric_b * widen(velocity[1])
        + metric_c * widen(velocity[2])
    )
    coupled = density_f * gradient[0] + heat_ratio * pressure_f * gradient[4]
    turned = (metric_a * gradient[1] + metric_b * gradient[2] + metric_c * gradient[3]) / density_f
    return [
        contravariant * gradient[0],
        contravariant * gradient[1] + metric_a * coupled,
        contravariant * gradient[2] + metric_b * coupled,
        contravariant * gradient[3] + metric_c * coupled,
        contravariant * gradient[4] + turned,
    ]


def face_patches(source_field):
    pieces = []
    for surface in (
        source_field[:, :, 0, :],
        source_field[:, :, -1, :],
        source_field[:, :, :, 0],
        source_field[:, :, :, -1],
    ):
        fields, row_count, length = surface.shape
        grouped = surface.reshape(fields, row_count, length // PW, PW)
        pieces.append(jnp.transpose(grouped, (2, 0, 1, 3)))
    return jnp.concatenate(pieces, axis=0)


def body(adjoint, density, velocity, pressure, metrics, links):
    highest = lax.Precision.HIGHEST
    field_bf = adjoint[:, 0]
    density_f = widen(density[0])
    velocity_b = velocity[:, 0]
    pressure_f = widen(pressure[0])
    metric_b = metrics[:, 0]
    field_count, local_cells, y_cells, z_cells = field_bf.shape
    local_inverse = line_tables(local_cells)[0]
    cross_table = line_tables(y_cells)[1]
    depth_table = line_tables(z_cells)[1]
    padded = extended(field_bf, (("ax", 1),), 2).astype(jnp.float32)
    stencil_sum = near_coef * (padded[:, 3 : local_cells + 3] - padded[:, 1 : local_cells + 1])
    stencil_sum = stencil_sum + far_coef * (
        padded[:, 4 : local_cells + 4] - padded[:, 0:local_cells]
    )
    batch_inverse = jnp.broadcast_to(local_inverse, (field_count, local_cells, local_cells))
    partial_value = lax.dot_general(
        batch_inverse,
        stencil_sum.reshape(field_count, local_cells, y_cells * z_cells),
        (((2,), (1,)), ((0,), (0,))),
        precision=highest,
    )
    partial_value = partial_value.reshape(field_count, local_cells, y_cells, z_cells)
    first_end = partial_value[:, 0]
    last_end = partial_value[:, -1]
    corner_first = local_inverse[0, 0]
    corner_last = local_inverse[-1, -1]
    segment = lax.axis_index("ax")
    segments = lax.axis_size("ax")
    line_ends = jnp.stack([first_end, last_end], axis=1)
    beside_all = extended(shortened(line_ends), (("ax", 1),), 1).astype(line_ends.dtype)
    before_last = beside_all[:, 0]
    after_first = beside_all[:, 3]
    shared = 1.0 - lhs_alpha * lhs_alpha * corner_first * corner_last
    left_value = jnp.where(
        segment > 0, (before_last - lhs_alpha * corner_last * first_end) / shared, 0.0
    )
    next_last = (last_end - lhs_alpha * corner_last * after_first) / shared
    right_value = jnp.where(
        segment < segments - 1, after_first - lhs_alpha * corner_first * next_last, 0.0
    )
    grad_x = partial_value - lhs_alpha * (
        left_value[:, None] * local_inverse[:, 0][None, :, None, None]
        + right_value[:, None] * local_inverse[:, -1][None, :, None, None]
    )
    field_rows = widen(field_bf).reshape(field_count * local_cells, y_cells, z_cells)
    batch_cross = jnp.broadcast_to(cross_table, (field_count * local_cells, y_cells, y_cells))
    grad_y = lax.dot_general(
        batch_cross, field_rows, (((2,), (1,)), ((0,), (0,))), precision=highest
    )
    grad_y = grad_y.reshape(field_count, local_cells, y_cells, z_cells)
    grad_z = jnp.dot(widen(field_bf).reshape(-1, z_cells), depth_table.T, precision=highest)
    grad_z = grad_z.reshape(field_count, local_cells, y_cells, z_cells)
    parts_x = flux_parts(grad_x, metric_b[0:3], density_f, velocity_b, pressure_f)
    parts_y = flux_parts(grad_y, metric_b[3:6], density_f, velocity_b, pressure_f)
    parts_z = flux_parts(grad_z, metric_b[6:9], density_f, velocity_b, pressure_f)
    own_faces = face_patches(field_bf)
    patch_count = own_faces.shape[0]
    flat_faces = own_faces.reshape(patch_count, -1)
    own_block = lax.axis_index("blk")
    own_links = lax.dynamic_index_in_dim(links, own_block, 1, keepdims=False)
    source = own_links[0]
    source_face = own_links[1]
    reversed_flag = own_links[2]
    patch_ids = jnp.arange(patch_count, dtype=jnp.int32)
    segment_faces = lax.all_gather(flat_faces[None], "blk", axis=0, tiled=True)
    count_here = segment_faces.shape[0]
    block_ids = jnp.arange(count_here, dtype=jnp.int32)
    selector = (source[:, None, None] == block_ids[None, :, None]) & (
        source_face[:, None, None] == patch_ids[None, None, :]
    )
    selector = selector.astype(jnp.bfloat16).reshape(patch_count, count_here * patch_count)
    gathered = segment_faces.reshape(count_here * patch_count, -1)
    received = jnp.dot(selector, gathered, preferred_element_type=jnp.float32)
    received = received.reshape(own_faces.shape)
    received = jnp.where((reversed_flag == 1)[:, None, None, None], received[..., ::-1], received)
    penalty = jnp.where(
        (source >= 0)[:, None, None, None],
        penalty_weight * (received - own_faces.astype(jnp.float32)),
        0.0,
    )
    z_parts = z_cells // PW
    y_parts = y_cells // PW

    def unfold(stacked, length):
        return jnp.transpose(stacked, (1, 2, 0, 3)).reshape(field_count, local_cells, length)

    plane_low_y = unfold(penalty[:z_parts], z_cells)
    plane_high_y = unfold(penalty[z_parts : 2 * z_parts], z_cells)
    plane_low_z = unfold(penalty[2 * z_parts : 2 * z_parts + y_parts], y_cells)
    plane_high_z = unfold(penalty[2 * z_parts + y_parts :], y_cells)
    y_index = jnp.arange(y_cells, dtype=jnp.int32)[:, None]
    z_index = jnp.arange(z_cells, dtype=jnp.int32)[None, :]
    components = []
    for component in range(5):
        total = parts_x[component] + parts_y[component] + parts_z[component]
        total = total + jnp.where(y_index == 0, plane_low_y[component][:, None, :], 0.0)
        total = total + jnp.where(y_index == y_cells - 1, plane_high_y[component][:, None, :], 0.0)
        total = total + jnp.where(z_index == 0, plane_low_z[component][:, :, None], 0.0)
        total = total + jnp.where(z_index == z_cells - 1, plane_high_z[component][:, :, None], 0.0)
        components.append(total.astype(jnp.bfloat16))
    return jnp.stack(components)[:, None]


def solution(mesh):
    in_specs = (
        P(None, "blk", "ax", None, None),
        P("blk", "ax", None, None),
        P(None, "blk", "ax", None, None),
        P("blk", "ax", None, None),
        P(None, "blk", "ax", None, None),
        P(),
    )
    out_specs = P(None, "blk", "ax", None, None)
    return jax.shard_map(body, mesh=mesh, in_specs=in_specs, out_specs=out_specs, check_vma=False)
```

profile of v0, /device:TPU:0, one launch (start us, length us, event | category | flops | bytes accessed | tf_op | source)
XLA Modules:
  0.0 976.7 jit_solution(7459704128567540675)
XLA Ops:
  6.5 11.5 %copy.126 = bf16[5,1,64,64,128]{2,4,0,3,1:T(8,128)(2,1)} copy(bf16[5,1,64,64,128]{4,3,2,1,0:T(8,128)(2,1)} %param.10) | data formatting | bytes 10485760 | tf_op args[0]
  18.1 18.5 %fusion.715 = (bf16[5,2,64,128]{1,3,0,2:T(8,128)(2,1)}, bf16[5,2,64,128]{1,3,0,2:T(8,128)(2,1)}) fusion(bf16[5,64,64,128]{1,3,0,2:T(8,128)(2,1)} %bitcast.2977), kind=kLoop, calls=%fused_computation.1107 | loop fusion | bytes 655360 | tf_op jit(solution)/shard_map/slice | solution.py:21
  36.6 7.9 copy.127
  44.5 4.9 collective-permute-start
  49.4 7.9 copy.128
  120.4 26.4 %subtract_divide_fusion.41 = (f32[1,64]{1,0:T(1,128)S(1)}, f32[1,64]{1,0:T(1,128)S(1)}, f32[1,64]{1,0:T(1,128)S(1)}, f32[1,64]{1,0:T(1,128)S(1)}, f32[1,64]{1,0:...) fusion(f32[64,64]{1,0:T(8,128)S(1)} %fusion.243, ...), kind=kLoop, calls=%fused_computation.1000 | loop fusion | flops 7872 | bytes 21576 | tf_op jit(solution)/shard_map/eval_jaxpr/div | solution.py:51
  174.5 40.4 %fusion.476 = (f32[1,64]{1,0:T(1,128)}, f32[64]{0:T(128)S(1)}, f32[64]{0:T(128)}, f32[64]{0:T(128)}, f32[64]{0:T(128)S(1)}, /*index=5*/f32[64]{0:T(128)}, f32[64...) fusion(f32[]{:T(128)S(6)} %div.27235, ...), kind=kLoop, calls=%fused_computation.1064 | loop fusion | flops 12224 | bytes 27644 | tf_op jit(solution)/shard_map/while/body/broadcast_in_dim | solution.py:51
  214.8 40.3 %fusion.486 = (f32[1,64]{1,0:T(1,128)}, f32[64]{0:T(128)S(1)}, f32[64]{0:T(128)}, f32[64]{0:T(128)}, f32[64]{0:T(128)S(1)}, /*index=5*/f32[64]{0:T(128)}, f32[64...) fusion(f32[]{:T(128)S(6)} %div.27235, ...), kind=kLoop, calls=%fused_computation.1074 | loop fusion | flops 12224 | bytes 27644 | tf_op jit(solution)/shard_map/while/body/broadcast_in_dim | solution.py:51
  255.2 26.5 %subtract_divide_fusion = (f32[1,64]{1,0:T(1,128)}, f32[1,64]{1,0:T(1,128)}, f32[1,64]{1,0:T(1,128)}, f32[1,64]{1,0:T(1,128)}, f32[1,64]{1,0:T(1,128)}, /*index=...) fusion(f32[64,64]{1,0:T(8,128)S(1)} %multiply_add_fusion.1, ...), kind=kLoop, calls=%fused_computation.897 | loop fusion | flops 7872 | bytes 21576 | tf_op jit(solution)/shard_map/eval_jaxpr/div | solution.py:51
  284.9 195.8 %while.8 = (s32[]{:T(128)}, f32[]{:T(128)}, f32[128]{0:T(128)S(1)}, f32[3,32]{1,0:T(4,128)S(1)}, f32[3,32,128]{2,1,0:T(8,128)S(1)}, /*index=5*/f32[3,32]{1,0:T(4...) while((s32[]{:T(128)}, f32[]{:T(128)}, ...), condition=%wide.region_1.2_spmd, body=%wide.region_0.1_spmd.sunk | while | flops 12417 | bytes 103653 | solution.py:54
  328.4 20.2 %fusion.751 = (f32[128]{0:T(128)S(1)}, f32[128]{0:T(128)S(1)}, f32[128]{0:T(128)S(1)}, f32[128]{0:T(128)S(1)}, f32[128]{0:T(128)S(1)}, /*index=5*/f32[128]{0:T(1...) fusion(f32[3,32,128]{2,1,0:T(8,128)S(1)} %get-tuple-element.155, ...), kind=kLoop, calls=%fused_computation.40.clone.1 | loop fusion | flops 12288 | bytes 33664 | tf_op jit(solution)/shard_map/while/body/eval_jaxpr/div | solution.py:54
  393.5 20.2 %fusion.751 = (f32[128]{0:T(128)S(1)}, f32[128]{0:T(128)S(1)}, f32[128]{0:T(128)S(1)}, f32[128]{0:T(128)S(1)}, f32[128]{0:T(128)S(1)}, /*index=5*/f32[128]{0:T(1...) fusion(f32[3,32,128]{2,1,0:T(8,128)S(1)} %get-tuple-element.155, ...), kind=kLoop, calls=%fused_computation.40.clone.1 | loop fusion | flops 12288 | bytes 33664 | tf_op jit(solution)/shard_map/while/body/eval_jaxpr/div | solution.py:54
  458.7 20.2 %fusion.751 = (f32[128]{0:T(128)S(1)}, f32[128]{0:T(128)S(1)}, f32[128]{0:T(128)S(1)}, f32[128]{0:T(128)S(1)}, f32[128]{0:T(128)S(1)}, /*index=5*/f32[128]{0:T(1...) fusion(f32[3,32,128]{2,1,0:T(8,128)S(1)} %get-tuple-element.155, ...), kind=kLoop, calls=%fused_computation.40.clone.1 | loop fusion | flops 12288 | bytes 33664 | tf_op jit(solution)/shard_map/while/body/eval_jaxpr/div | solution.py:54
  521.8 19.2 %fusion.307 = (f32[128]{0:T(128)S(1)}, f32[128]{0:T(128)S(1)}, f32[128]{0:T(128)S(1)}, f32[128]{0:T(128)S(1)}, f32[128]{0:T(128)S(1)}, /*index=5*/f32[128]{0:T(1...) fusion(f32[128,128]{1,0:T(8,128)S(1)} %multiply_add_fusion, ...), kind=kLoop, calls=%fused_computation.520 | loop fusion | flops 11904 | bytes 32504 | tf_op jit(solution)/shard_map/eval_jaxpr/div | solution.py:54
  541.1 64.5 %while.9 = (s32[]{:T(128)}, f32[128]{0:T(128)S(1)}, f32[3,32,128]{2,1,0:T(8,128)S(1)}, f32[3,32,128]{2,1,0:T(8,128)S(1)}, f32[3,32]{1,0:T(4,128)S(1)}, /*index=5...) while((s32[]{:T(128)}, f32[128]{0:T(128)S(1)}, ...), condition=%wide.region_3.4_spmd, body=%wide.region_2.3_spmd.sunk | while | flops 8226 | bytes 101333 | solution.py:54
  542.6 19.9 %fusion.754 = (f32[128]{0:T(128)S(1)}, f32[128]{0:T(128)S(1)}, f32[128]{0:T(128)S(1)}, f32[128]{0:T(128)S(1)}, f32[128]{0:T(128)S(1)}, /*index=5*/f32[128]{0:T(1...) fusion(f32[3,32,128]{2,1,0:T(8,128)S(1)} %get-tuple-element.166, ...), kind=kLoop, calls=%fused_computation.168.clone.1 | loop fusion | flops 8192 | bytes 33536 | tf_op jit(solution)/shard_map/while/body/eval_jaxpr/sub | solution.py:54
  564.1 19.9 %fusion.754 = (f32[128]{0:T(128)S(1)}, f32[128]{0:T(128)S(1)}, f32[128]{0:T(128)S(1)}, f32[128]{0:T(128)S(1)}, f32[128]{0:T(128)S(1)}, /*index=5*/f32[128]{0:T(1...) fusion(f32[3,32,128]{2,1,0:T(8,128)S(1)} %get-tuple-element.166, ...), kind=kLoop, calls=%fused_computation.168.clone.1 | loop fusion | flops 8192 | bytes 33536 | tf_op jit(solution)/shard_map/while/body/eval_jaxpr/sub | solution.py:54
  585.6 19.9 %fusion.754 = (f32[128]{0:T(128)S(1)}, f32[128]{0:T(128)S(1)}, f32[128]{0:T(128)S(1)}, f32[128]{0:T(128)S(1)}, f32[128]{0:T(128)S(1)}, /*index=5*/f32[128]{0:T(1...) fusion(f32[3,32,128]{2,1,0:T(8,128)S(1)} %get-tuple-element.166, ...), kind=kLoop, calls=%fused_computation.168.clone.1 | loop fusion | flops 8192 | bytes 33536 | tf_op jit(solution)/shard_map/while/body/eval_jaxpr/sub | solution.py:54
  617.6 2.8 fusion.505
  646.8 6.2 convolution_bitcast_fusion
  653.1 3.5 fusion.713
  677.4 14.3 %fusion.475 = (f32[1,64]{1,0:T(1,128)S(1)}, f32[64]{0:T(128)S(1)}) fusion(f32[64]{0:T(128)} %get-tuple-element.524, f32[64]{0:T(128)} %get-tuple-element.523, f32[64]{0:T(128)} %get-tuple-element.522, f32[64]{0:T(128)} %get-tuple-element.521, f32[64]{0:T(128)} %get-tuple-element.520, f32[64]{0:T(128)} %get-tuple-element.519, f32[64]{0:T(128)} %get-tuple-element.518, ...), kind=kLoop, calls=%fused_computation.1062 | loop fusion | flops 9600 | bytes 12628 | tf_op jit(solution)/shard_map/broadcast_in_dim | solution.py:51
  691.7 15.8 %multiply_subtract_fusion.1 = (f32[1,64]{1,0:T(1,128)S(1)}, f32[1,64]{1,0:T(1,128)}, f32[1,64]{1,0:T(1,128)}, f32[1,64]{1,0:T(1,128)}, f32[1,64]{1,0:T(1,128)}, ...) fusion(f32[1,64]{1,0:T(1,128)S(1)} %get-tuple-element.625, ...), kind=kLoop, calls=%fused_computation.855 | loop fusion | flops 12160 | bytes 27304 | tf_op jit(solution)/shard_map/eval_jaxpr/sub | solution.py:51
  707.6 5.6 concatenate.70
  713.5 8.5 fusion.163
  722.4 13.5 %fusion.474 = (f32[1,64]{1,0:T(1,128)S(1)}, f32[64]{0:T(128)S(1)}) fusion(f32[64]{0:T(128)S(1)} %copy-done.42, f32[64]{0:T(128)S(1)} %copy-done.41, f32[64]{0:T(128)S(1)} %copy-done.40, f32[64]{0:T(128)S(1)} %copy-done.39, f32[64]{0:T(128)S(1)} %copy-done.38, f32[64]{0:T(128)S(1)} %copy-done.37, f32[64]{0:T(128)S(1)} %copy-done.36, f32[64]{0:T(128)S(1)} %copy-done.35, ...), kind=kLoop, calls=%fused_computation.1061 | loop fusion | flops 9600 | bytes 12628 | tf_op jit(solution)/shard_map/broadcast_in_dim | solution.py:51
  736.0 15.0 %multiply_subtract_fusion.63 = (f32[1,64]{1,0:T(1,128)S(1)}, f32[1,64]{1,0:T(1,128)S(1)}, f32[1,64]{1,0:T(1,128)S(1)}, f32[1,64]{1,0:T(1,128)}, f32[1,64]{1,0:T(...) fusion(f32[1,64]{1,0:T(1,128)S(1)} %get-tuple-element.480, ...), kind=kLoop, calls=%fused_computation.958 | loop fusion | flops 12160 | bytes 27304 | tf_op jit(solution)/shard_map/eval_jaxpr/sub | solution.py:51
  753.0 3.0 copy.132
  756.1 3.1 copy.151
  759.1 2.9 copy.152
  762.1 2.9 copy.161
  769.9 6.8 copy.129
  776.8 6.9 copy.130
  783.7 21.8 %maximum_convert_fusion = f32[5,68,64,128]{1,3,0,2:T(8,128)} fusion(bf16[5,2,64,128]{1,3,0,2:T(8,128)(2,1)} %copy.130, bf16[5,64,64,128]{1,3,0,2:T(8,128)(2,1)} %bitcast.2980, bf16[5,2,64,128]{1,3,0,2:T(8,128)(2,1)} %copy.129), kind=kLoop, calls=%fused_computation.235 | loop fusion | flops 16711680 | bytes 16711680 | tf_op jit(solution)/shard_map/convert_element_type | solution.py:107
  805.5 36.6 %fusion.161 = f32[5,64,64,128]{1,3,0,2:T(8,128)} fusion(f32[5,68,64,128]{1,3,0,2:T(8,128)} %maximum_convert_fusion), kind=kLoop, calls=%fused_computation.232 | loop fusion | flops 13107200 | bytes 52428800 | tf_op jit(solution)/shard_map/add | solution.py:109
  842.0 16.8 %copy.131 = f32[5,64,64,128]{3,2,1,0:T(8,128)} copy(f32[5,64,64,128]{1,3,0,2:T(8,128)} %fusion.161) | data formatting | bytes 20971520 | tf_op jit(solution)/shard_map/add | solution.py:109
  858.8 11.6 %reshape.2774 = f32[5,64,8192]{2,1,0:T(8,128)} reshape(f32[5,64,64,128]{3,2,1,0:T(8,128)} %copy.131) | data formatting | bytes 20971520 | tf_op jit(solution)/shard_map/reshape | solution.py:115
  870.4 12.0 %fusion.232 = f32[5,64,8192]{2,1,0:T(8,128)S(1)} fusion(f32[5,64,8192]{2,1,0:T(8,128)} %reshape.2774, f32[64,64]{1,0:T(8,128)S(1)} %concatenate.67), kind=kOutput, calls=%fused_computation.377 | convolution fusion | flops 2013265920 | bytes 20987904 | tf_op jit(solution)/shard_map/dot_general | solution.py:113
  882.5 6.1 copy.189
  889.6 4.5 collective-permute-start.2
  896.2 4.3 collective-permute-done.3
  901.6 10.9 %multiply_subtract_fusion = f32[5,64,64,128]{3,2,1,0:T(8,128)} fusion(f32[64]{0:T(128)S(1)} %get-tuple-element.239, f32[5,64,128]{2,1,0:T(8,128)S(1)} %get-tuple-element.790, f32[64]{0:T(128)S(1)} %get-tuple-element.238, f32[5,64,128]{2,1,0:T(8,128)S(1)} %get-tuple-element.789, f32[5,64,64,128]{3,2,1,0:T(8,128)} %bitcast.2990), kind=kLoop, calls=%fused_computation.236 | loop fusion | flops 13107200 | bytes 21299712 | tf_op jit(solution)/shard_map/sub | solution.py:138
  912.4 3.1 copy.141
  922.4 10.1 %bitcast_dynamic-update-slice_fusion.6 = (bf16[5,64,64,128]{3,2,1,0:T(8,128)(2,1)}, f32[64,64,128]{2,1,0:T(8,128)S(1)}, f32[64,64,128]{2,1,0:T(8,128)S(1)}, f32[64,64,128]{2,1,0:T(8,128)}) fusion(f32[64,64]{1,0:T(8,128)S(1)} %copy.150, f32[64,64,128]{2,1,0:T(8,128)} %bitcast.2991, f32[320,64,128]{2,1,0:T(8,128)} %fusion.163, ...), kind=kLoop, calls=%fused_computation.344 | loop fusion | flops 21495808 | bytes 26313088
  933.4 10.5 %bitcast_dynamic-update-slice_fusion.5 = (bf16[5,64,64,128]{3,2,1,0:T(8,128)(2,1)}, f32[64,64,128]{2,1,0:T(8,128)}, f32[64,64,128]{2,1,0:T(8,128)}, f32[64,64,128]{2,1,0:T(8,128)}) fusion(bf16[5,64,64,128]{3,2,1,0:T(8,128)(2,1)} %get-tuple-element.334, f32[64,64,128]{2,1,0:T(8,128)} %get-tuple-element.337, f32[64,64,128]{2,1,0:T(8,128)} %bitcast.2993, ...), kind=kLoop, calls=%fused_computation.343 | loop fusion | flops 18350080 | bytes 37847424
  943.9 8.1 bitcast_dynamic-update-slice_fusion.4
  952.1 7.5 bitcast_dynamic-update-slice_fusion.3
  959.6 9.8 %bitcast_dynamic-update-slice_fusion.2 = bf16[5,64,64,128]{3,2,1,0:T(8,128)(2,1)} fusion(bf16[5,64,64,128]{3,2,1,0:T(8,128)(2,1)} %bitcast_dynamic-update-slice_fusion.3, f32[64,64]{1,0:T(8,128)S(1)} %copy-done.7, pred[128]{0:T(512)(128)(4,1)S(1)} %get-tuple-element.1053, f32[64,64]{1,0:T(8,128)S(1)} %copy-done.6, ...), kind=kLoop, calls=%fused_computation.340 | loop fusion | flops 23592960 | bytes 43090304 | tf_op jit(solution)/shard_map/stack | solution.py:198
  (383 shorter events, 108.9 us)
Async XLA Ops:
  6.5 905.9 %all-gather.2.cloned.1.call-start = ((), (), s32[]{:S(2)}) async-start(), calls=%async_computation | async-start | bytes 2211840 | tf_op jit(solution)/shard_map/all_gather | solution.py:162
  44.5 725.5 %collective-permute-start = (bf16[5,2,64,128]{3,2,1,0:T(8,128)(2,1)S(1)}, bf16[5,2,64,128]{3,2,1,0:T(8,128)(2,1)S(1)}, u32[]{:S(2)}, u32[]{:S(2)}) collective-permute-start(bf16[5,2,64,128]{3,2,1,0:T(8,128)(2,1)S(1)} %copy.127), channel_id=1, source_target_pairs={{0,1},{1,2},{2,3},{4,5},{5,6},{6,7},{8,9},{9,10},{10,11},{12,13},{... | collective-permute-start | bytes 491528 | tf_op jit(solution)/shard_map/ppermute | solution.py:24
  57.3 719.5 %collective-permute-start.1 = (bf16[5,2,64,128]{3,2,1,0:T(8,128)(2,1)S(1)}, bf16[5,2,64,128]{3,2,1,0:T(8,128)(2,1)S(1)}, u32[]{:S(2)}, u32[]{:S(2)}) collective-permute-start(bf16[5,2,64,128]{3,2,1,0:T(8,128)(2,1)S(1)} %copy.128), channel_id=1, source_target_pairs={{1,0},{2,1},{3,2},{5,4},{6,5},{7,6},{9,8},{10,9},{11,10},{13,12},{... | collective-permute-start | bytes 491528 | tf_op jit(solution)/shard_map/ppermute | solution.py:26
  480.8 124.8 %copy-start.2 = (f32[3,32,128]{2,1,0:T(8,128)}, f32[3,32,128]{2,1,0:T(8,128)S(1)}, u32[]{:S(2)}) copy-start(f32[3,32,128]{2,1,0:T(8,128)S(1)} %get-tuple-element.232) | copy-start | bytes 147460
  653.1 22.6 %copy-start.82 = (f32[64]{0:T(128)S(1)}, f32[64]{0:T(128)}, u32[]{:S(2)}) copy-start(f32[64]{0:T(128)} %get-tuple-element.355) | copy-start | bytes 772
  713.2 9.0 copy-start.22
  713.2 9.0 copy-start.23
  713.2 9.0 copy-start.24
  713.2 9.0 copy-start.25
  713.2 9.0 copy-start.26
  713.3 9.0 copy-start.27
  713.3 9.0 copy-start.28
  713.3 9.0 copy-start.29
  713.3 9.0 copy-start.30
  713.3 9.0 copy-start.31
  713.3 9.0 copy-start.32
  713.3 9.0 copy-start.33
  713.3 9.0 copy-start.34
  713.3 9.0 copy-start.35
  713.3 9.0 copy-start.36
  713.4 9.0 copy-start.37
  713.4 9.0 copy-start.38
  713.4 9.0 copy-start.39
  713.4 9.0 copy-start.40
  713.4 9.0 copy-start.41
  713.4 9.0 copy-start.42
  713.4 22.5 %copy-start.8 = (f32[1,64]{1,0:T(1,128)S(1)}, f32[1,64]{1,0:T(1,128)}, u32[]{:S(2)}) copy-start(f32[1,64]{1,0:T(1,128)} %get-tuple-element.467) | copy-start | bytes 772
  713.4 22.5 %copy-start.9 = (f32[1,64]{1,0:T(1,128)S(1)}, f32[1,64]{1,0:T(1,128)}, u32[]{:S(2)}) copy-start(f32[1,64]{1,0:T(1,128)} %get-tuple-element.468) | copy-start | bytes 772
  713.4 22.5 %copy-start.10 = (f32[1,64]{1,0:T(1,128)S(1)}, f32[1,64]{1,0:T(1,128)}, u32[]{:S(2)}) copy-start(f32[1,64]{1,0:T(1,128)} %get-tuple-element.469) | copy-start | bytes 772
  713.4 22.5 %copy-start.11 = (f32[1,64]{1,0:T(1,128)S(1)}, f32[1,64]{1,0:T(1,128)}, u32[]{:S(2)}) copy-start(f32[1,64]{1,0:T(1,128)} %get-tuple-element.470) | copy-start | bytes 772
  713.5 22.5 %copy-start.12 = (f32[1,64]{1,0:T(1,128)S(1)}, f32[1,64]{1,0:T(1,128)}, u32[]{:S(2)}) copy-start(f32[1,64]{1,0:T(1,128)} %get-tuple-element.471) | copy-start | bytes 772
  713.5 22.5 %copy-start.13 = (f32[1,64]{1,0:T(1,128)S(1)}, f32[1,64]{1,0:T(1,128)}, u32[]{:S(2)}) copy-start(f32[1,64]{1,0:T(1,128)} %get-tuple-element.472) | copy-start | bytes 772
  713.5 22.5 %copy-start.14 = (f32[1,64]{1,0:T(1,128)S(1)}, f32[1,64]{1,0:T(1,128)}, u32[]{:S(2)}) copy-start(f32[1,64]{1,0:T(1,128)} %get-tuple-element.473) | copy-start | bytes 772
  713.5 22.5 %copy-start.15 = (f32[1,64]{1,0:T(1,128)S(1)}, f32[1,64]{1,0:T(1,128)}, u32[]{:S(2)}) copy-start(f32[1,64]{1,0:T(1,128)} %get-tuple-element.474) | copy-start | bytes 772
  713.5 22.5 %copy-start.16 = (f32[1,64]{1,0:T(1,128)S(1)}, f32[1,64]{1,0:T(1,128)}, u32[]{:S(2)}) copy-start(f32[1,64]{1,0:T(1,128)} %get-tuple-element.475) | copy-start | bytes 772
  713.5 22.5 %copy-start.17 = (f32[1,64]{1,0:T(1,128)S(1)}, f32[1,64]{1,0:T(1,128)}, u32[]{:S(2)}) copy-start(f32[1,64]{1,0:T(1,128)} %get-tuple-element.476) | copy-start | bytes 772
  713.5 22.5 %copy-start.18 = (f32[1,64]{1,0:T(1,128)S(1)}, f32[1,64]{1,0:T(1,128)}, u32[]{:S(2)}) copy-start(f32[1,64]{1,0:T(1,128)} %get-tuple-element.477) | copy-start | bytes 772
  713.5 22.5 %copy-start.19 = (f32[1,64]{1,0:T(1,128)S(1)}, f32[1,64]{1,0:T(1,128)}, u32[]{:S(2)}) copy-start(f32[1,64]{1,0:T(1,128)} %get-tuple-element.478) | copy-start | bytes 772
  713.5 22.5 %copy-start.20 = (f32[1,64]{1,0:T(1,128)S(1)}, f32[1,64]{1,0:T(1,128)}, u32[]{:S(2)}) copy-start(f32[1,64]{1,0:T(1,128)} %get-tuple-element.479) | copy-start | bytes 772
  889.6 6.6 collective-permute-start.2
  894.2 6.3 collective-permute-start.3
  922.4 10.1 %slice-start = ((s8[10485760]{0:T(1024)(128)(4,1)}), s8[4194304]{0:T(1024)(128)(4,1)S(1)}, s32[]{:S(2)}) async-start(s8[10485760]{0:T(1024)(128)(4,1)} %bitcast.2981), calls=%async_computation.1 | async-start | bytes 8388608
  922.4 10.1 %slice-start.1 = ((s8[10485760]{0:T(1024)(128)(4,1)}), s8[4194304]{0:T(1024)(128)(4,1)S(1)}, s32[]{:S(2)}) async-start(s8[10485760]{0:T(1024)(128)(4,1)} %bitcast.2981), calls=%async_computation.2 | async-start | bytes 8388608
  922.4 10.8 %slice-start.2 = ((s8[10485760]{0:T(1024)(128)(4,1)}), s8[2097152]{0:T(1024)(128)(4,1)S(1)}, s32[]{:S(2)}) async-start(s8[10485760]{0:T(1024)(128)(4,1)} %bitcast.2981), calls=%async_computation.3 | async-start | bytes 4194304
  922.4 11.0 %copy-start.1 = (bf16[1,64,64,128]{3,2,1,0:T(8,128)(2,1)S(1)}, bf16[1,64,64,128]{3,2,1,0:T(8,128)(2,1)}, u32[]{:S(2)}) copy-start(bf16[1,64,64,128]{3,2,1,0:T(8,128)(2,1)} %param.11) | copy-start | bytes 3145732
  943.9 8.1 copy-start
  943.9 15.7 %slice-start.3 = ((s8[10485760]{0:T(1024)(128)(4,1)}), s8[4194304]{0:T(1024)(128)(4,1)S(1)}, s32[]{:S(2)}) async-start(s8[10485760]{0:T(1024)(128)(4,1)} %bitcast.2983), calls=%async_computation.4 | async-start | bytes 8388608
  943.9 15.7 %slice-start.4 = ((s8[10485760]{0:T(1024)(128)(4,1)}), s8[4194304]{0:T(1024)(128)(4,1)S(1)}, s32[]{:S(2)}) async-start(s8[10485760]{0:T(1024)(128)(4,1)} %bitcast.2983), calls=%async_computation.5 | async-start | bytes 8388608
  (49 other events, 148.7 us)
Sparse Core Ops, SparseCore 0:
  62.9 29.6 all-gather.1
where the time goes:
time: 993 us; the launch traced here: 977 us
  other arithmetic  510 us (51%)
  local copies, waits for them, and re-layouts  162 us (16%)
  between operations  135 us (14%)
  loops' own time  124 us (12%)
  matrix products  28.1 us (3%)
  starting transfers between devices  12.1 us (1%)
    broadcast_in_dim x21, other arithmetic, line_tables(): lax.linalg.tridiagonal_solve(sub_diag, middle, super_diag, jnp.eye(line_c...  127 us
    another operation x2, loops' own time, line_tables(): lax.linalg.tridiagonal_solve(sub_diag, middle, super_diag, stencil)  124 us
    div x4, other arithmetic, line_tables(): lax.linalg.tridiagonal_solve(sub_diag, middle, super_diag, stencil)  79.7 us
    sub x3, other arithmetic, line_tables(): lax.linalg.tridiagonal_solve(sub_diag, middle, super_diag, stencil)  59.7 us
    div x2, other arithmetic, line_tables(): lax.linalg.tridiagonal_solve(sub_diag, middle, super_diag, jnp.eye(line_c...  52.9 us
    broadcast_in_dim x17, other arithmetic, line_tables(): lax.linalg.tridiagonal_solve(sub_diag, middle, super_diag, stencil)  41.1 us
    add x1, other arithmetic, body(): stencil_sum + far_coef * (padded[:, 4:local_cells + 4] - padded[:, 0:loca...  36.6 us
    unnamed x6, other arithmetic  36.1 us
  transfers between devices with their start and end apart: 5, of which 1 were waited for; matrix products, arithmetic and copies ran while one was open for 62% of the time, Pallas kernels for 0%

commit v1 on v0

v1 whole, which is shorter than its diff:
```python
import functools

import jax
import jax.numpy as jnp
import numpy as np
from jax import lax
from jax.experimental import pallas as pl
from jax.experimental.pallas import tpu as pltpu
from jax.sharding import PartitionSpec as P

PW = 8
FIELDS = 5

lhs_alpha = 1.0 / 3.0
near_coef = 7.0 / 9.0
far_coef = 1.0 / 36.0
heat_ratio = 1.4
penalty_weight = 1.0

bf16 = jnp.bfloat16
f32 = jnp.float32


def tables(n):
    lhs = np.eye(n) + lhs_alpha * (np.eye(n, k=1) + np.eye(n, k=-1))
    rhs = near_coef * (np.eye(n, k=1) - np.eye(n, k=-1))
    rhs = rhs + far_coef * (np.eye(n, k=2) - np.eye(n, k=-2))
    inverse = np.linalg.inv(lhs)
    return inverse, inverse @ rhs


def split(table):
    high = table.astype(bf16)
    low = (table - high.astype(np.float64)).astype(bf16)
    return high, low


def sweep_coefs(n):
    weight = np.zeros(n)
    upper = np.zeros(n)
    for i in range(n):
        weight[i] = 1.0 / (1.0 - lhs_alpha * (upper[i - 1] if i else 0.0))
        upper[i] = lhs_alpha * weight[i]
    return weight, upper


def pack_kernel(nx, ny, nz, end_rows, target_ref, adj_ref, send_ref, ends_ref, yface, zface):
    f = pl.program_id(0)
    lane = lax.broadcasted_iota(jnp.int32, (ny, nz), 1)
    first = jnp.zeros((ny, nz), f32)
    last = jnp.zeros((ny, nz), f32)
    sides = jnp.zeros((ny, nz), f32)
    for x in range(nx):
        slab = adj_ref[0, x].astype(f32)
        first = first + float(end_rows[0, x]) * slab
        last = last + float(end_rows[1, x]) * slab
        yface[f, x : x + 1, 0:nz] = slab[0:1]
        yface[f, x : x + 1, nz : 2 * nz] = slab[ny - 1 :]
        turned = pltpu.roll(slab, 2 * x + 1, 1)
        sides = jnp.where(lane // 2 == x, turned, sides)
    ends_ref[0, 0] = first
    ends_ref[0, 1] = last
    zface[f] = sides

    @pl.when(f == FIELDS - 1)
    def _():
        row = lax.broadcasted_iota(jnp.int32, (nz, 2 * nx), 0)
        col = lax.broadcasted_iota(jnp.int32, (nz, 2 * nx), 1)
        wanted = jnp.where(col < nx, 2 * col + 1, 2 * (col - nx))
        order = jnp.where(row == wanted, 1.0, 0.0).astype(bf16)
        low, high = [], []
        for g in range(FIELDS):
            sorted_side = jnp.dot(
                zface[g].astype(bf16), order, preferred_element_type=f32
            )
            low.append(sorted_side[:, :nx])
            high.append(sorted_side[:, nx:])
        cells = jnp.concatenate(
            [jnp.concatenate(low, axis=1), jnp.concatenate(high, axis=1)], axis=0
        ).astype(bf16)
        rows = send_ref.shape[0]
        slots = lax.broadcasted_iota(jnp.int32, (rows, 2 * nz + 2 * ny), 0)
        chosen = jnp.where(slots == target_ref[...], 1.0, 0.0).astype(bf16)
        packed = lax.dot_general(
            chosen[:, : 2 * nz],
            yface[...].reshape(FIELDS * nx, 2 * nz).astype(bf16),
            (((1,), (1,)), ((), ())),
            preferred_element_type=f32,
        )
        packed = packed + jnp.dot(chosen[:, 2 * nz :], cells, preferred_element_type=f32)
        send_ref[...] = packed.astype(bf16)


def main_kernel(
    nx, ny, nz, bx,
    upper_ref, adj_ref, edge_ref, recv_ref, ysrc_ref, zsrc_ref, ymask_ref, zmask_ref,
    dy_ref, dz_ref, rho_ref, vel_ref, prs_ref, met_ref,
    out_ref,
    sweep, ypen, zpen, carry, gyz,
):
    step = pl.program_id(0)
    block = pl.num_programs(0) - 1 - step
    weight, upper = sweep_coefs(nx)
    part = 32 if ny % 32 == 0 else ny

    @pl.when(step == 0)
    def _():
        rows = recv_ref.shape[0]
        received = recv_ref[...]
        slots = lax.broadcasted_iota(jnp.int32, (rows, 2 * nz), 0)
        ypick = jnp.where(slots == ysrc_ref[...], 1.0, 0.0).astype(bf16)
        ypen[...] = lax.dot_general(
            received, ypick, (((0,), (0,)), ((), ())), preferred_element_type=f32
        ).reshape(FIELDS, nx, 2 * nz)
        slots = lax.broadcasted_iota(jnp.int32, (2 * ny, rows), 1)
        zpick = jnp.where(slots == zsrc_ref[...], 1.0, 0.0).astype(bf16)
        zcells = jnp.dot(zpick, received, preferred_element_type=f32).astype(bf16)
        row = lax.broadcasted_iota(jnp.int32, (2 * nx, nz), 0)
        col = lax.broadcasted_iota(jnp.int32, (2 * nx, nz), 1)
        wanted = jnp.where(row < nx, 2 * row + 1, 2 * (row - nx))
        order = jnp.where(col == wanted, 1.0, 0.0).astype(bf16)
        for f in range(FIELDS):
            both = jnp.concatenate(
                [zcells[:ny, f * nx : (f + 1) * nx], zcells[ny:, f * nx : (f + 1) * nx]], axis=1
            )
            zpen[f] = jnp.dot(both, order, preferred_element_type=f32)

        def forward(index, state):
            f = index // (ny // part)
            at = pl.ds(pl.multiple_of((index % (ny // part)) * part, part), part)
            zero = jnp.zeros((part, nz), f32)
            window = [zero, zero, adj_ref[f, 0, at, :].astype(f32), adj_ref[f, 1, at, :].astype(f32)]
            before = zero
            for x in range(nx):
                ahead = adj_ref[f, x + 2, at, :].astype(f32) if x + 2 < nx else zero
                window.append(ahead)
                total = near_coef * (window[3] - window[1]) + far_coef * (window[4] - window[0])
                if x < 2:
                    total = total + edge_ref[f, x, at, :]
                elif x >= nx - 2:
                    total = total + edge_ref[f, x - nx + 4, at, :]
                before = float(weight[x]) * total - float(upper[x]) * before
                sweep[f, x, at, :] = before
                window = window[1:]
            return state

        lax.fori_loop(0, FIELDS * (ny // part), forward, 0)
        carry[...] = jnp.zeros_like(carry)

    chunk = 16 if ny % 16 == 0 else ny
    unroll = 2

    def one(j, slot):
        x = block * bx + j
        slabs = [adj_ref[f, x] for f in range(FIELDS)]
        tall = jnp.concatenate(slabs, axis=0)
        gyz[slot, 0] = jnp.dot(
            jnp.concatenate([tall, tall], axis=1), dz_ref[...], preferred_element_type=f32
        ).reshape(FIELDS, ny, nz)
        wide = jnp.concatenate(slabs, axis=1)
        across = jnp.dot(
            dy_ref[...], jnp.concatenate([wide, wide], axis=0), preferred_element_type=f32
        )
        for f in range(FIELDS):
            gyz[slot, 1, f] = across[:, f * nz : (f + 1) * nz]
        back = upper_ref[x]
        group = pl.ds(pl.multiple_of(block * bx, bx), bx)
        for y0 in range(0, ny, chunk):
            at = slice(y0, y0 + chunk)
            gx = []
            for f in range(FIELDS):
                value = sweep[f, x, at, :] - back * carry[f, at, :]
                carry[f, at, :] = value
                gx.append(value)
            gy = [gyz[slot, 1, f, at, :] for f in range(FIELDS)]
            gz = [gyz[slot, 0, f, at, :] for f in range(FIELDS)]
            rho = rho_ref[j, at, :].astype(f32)
            vel = [vel_ref[c, j, at, :].astype(f32) for c in range(3)]
            prs = heat_ratio * prs_ref[j, at, :].astype(f32)
            totals = [None] * FIELDS

            def add(i, value):
                totals[i] = value if totals[i] is None else totals[i] + value

            turned = None
            for d, g in enumerate((gx, gy, gz)):
                k = [met_ref[3 * d + c, j, at, :].astype(f32) for c in range(3)]
                speed = k[0] * vel[0] + k[1] * vel[1] + k[2] * vel[2]
                coupled = rho * g[0] + prs * g[4]
                for i in range(FIELDS):
                    add(i, speed * g[i])
                for i in range(3):
                    add(i + 1, k[i] * coupled)
                dot = k[0] * g[1] + k[1] * g[2] + k[2] * g[3]
                turned = dot if turned is None else turned + dot
            add(4, turned / rho)
            zmask = zmask_ref[at, :]
            for f in range(FIELDS):
                own = adj_ref[f, x, at, :].astype(f32)
                other = pltpu.roll(zpen[f, at, :], nz - 1 - 2 * x, 1)
                total = totals[f] + zmask * (other - own)
                if y0 == 0:
                    spot = lax.broadcasted_iota(jnp.int32, (chunk, nz), 0) == 0
                    near_rows = pltpu.roll(ypen[f, group, 0:nz], lax.rem(bx - j, bx), 0)
                    jump = jnp.concatenate([near_rows] * (chunk // bx), axis=0) - own
                    total = total + jnp.where(spot, ymask_ref[0:1, :] * jump, 0.0)
                if y0 + chunk == ny:
                    spot = lax.broadcasted_iota(jnp.int32, (chunk, nz), 0) == chunk - 1
                    near_rows = pltpu.roll(ypen[f, group, nz : 2 * nz], bx - 1 - j, 0)
                    jump = jnp.concatenate([near_rows] * (chunk // bx), axis=0) - own
                    total = total + jnp.where(spot, ymask_ref[1:2, :] * jump, 0.0)
                out_ref[f, j, at, :] = total.astype(bf16)

    def several(i, state):
        for u in range(unroll):
            one(bx - 1 - (i * unroll + u), u)
        return state

    lax.fori_loop(0, bx // unroll, several, 0)


def body(adjoint, density, velocity, pressure, metrics, links):
    adj = adjoint[:, 0]
    _, nx, ny, nz = adj.shape
    blocks, patches = links.shape[1:]
    blk_count = lax.axis_size("blk")
    segments = lax.axis_size("ax")
    segment = lax.axis_index("ax")
    me = lax.axis_index("blk")
    capacity = -(-patches // blocks)
    inverse, derivative = tables(nx)

    ups = [(i, i + 1) for i in range(segments - 1)]
    downs = [(i + 1, i) for i in range(segments - 1)]
    left_halo = lax.ppermute(adj[:, nx - 2 :], "ax", ups)
    right_halo = lax.ppermute(adj[:, :2], "ax", downs)

    source, face, turn = links[0], links[1], links[2]
    earlier = np.tril(np.ones((patches, patches), bool), -1)[None]
    same = (source[:, :, None] == source[:, None, :]) & earlier
    slot = jnp.sum(same.astype(jnp.int32), axis=2)
    place = jnp.arange(blocks, dtype=jnp.int32)[:, None] * capacity + slot
    mine = (source == me)[None] & (face[None] == jnp.arange(patches, dtype=jnp.int32)[:, None, None])
    slot_of = jnp.sum(jnp.where(mine, place[None] + 1, 0), axis=(1, 2)) - 1
    cell = jnp.arange(PW, dtype=jnp.int32)[None, :]
    target = jnp.where(slot_of[:, None] >= 0, slot_of[:, None] * PW + cell, -1).reshape(1, -1)
    own_source = lax.dynamic_index_in_dim(source, me, 0, keepdims=False)[:, None]
    own_slot = lax.dynamic_index_in_dim(slot, me, 0, keepdims=False)[:, None]
    own_turn = lax.dynamic_index_in_dim(turn, me, 0, keepdims=False)[:, None]
    origin = (own_source * capacity + own_slot) * PW + jnp.where(own_turn == 1, PW - 1 - cell, cell)
    origin = jnp.where(own_source >= 0, origin, -1).reshape(1, -1)
    live = penalty_weight * jnp.broadcast_to(
        (own_source >= 0).astype(f32), (patches, PW)
    ).reshape(-1)
    ymask = live[: 2 * nz].reshape(2, nz)
    zlive = live[2 * nz :].reshape(2, ny)
    column = jnp.arange(nz, dtype=jnp.int32)[None, :]
    zmask = jnp.where(column == 0, zlive[0][:, None], 0.0)
    zmask = zmask + jnp.where(column == nz - 1, zlive[1][:, None], 0.0)

    rows = blk_count * capacity * PW
    send, ends = pl.pallas_call(
        functools.partial(pack_kernel, nx, ny, nz, derivative[[0, nx - 1]]),
        grid=(FIELDS,),
        out_shape=(
            jax.ShapeDtypeStruct((rows, FIELDS * nx), bf16),
            jax.ShapeDtypeStruct((FIELDS, 2, ny, nz), f32),
        ),
        in_specs=[
            pl.BlockSpec((1, 2 * nz + 2 * ny), lambda f: (0, 0)),
            pl.BlockSpec((1, nx, ny, nz), lambda f: (f, 0, 0, 0)),
        ],
        out_specs=(
            pl.BlockSpec((rows, FIELDS * nx), lambda f: (0, 0)),
            pl.BlockSpec((1, 2, ny, nz), lambda f: (f, 0, 0, 0)),
        ),
        scratch_shapes=[
            pltpu.VMEM((FIELDS, nx, 2 * nz), f32),
            pltpu.VMEM((FIELDS, ny, nz), f32),
        ],
        compiler_params=pltpu.CompilerParams(vmem_limit_bytes=32 << 20),
        name="pack_faces",
    )(target, adj)

    recv = lax.all_to_all(
        send.reshape(blk_count, capacity * PW, FIELDS * nx), "blk", 0, 0, tiled=True
    ).reshape(rows, FIELDS * nx)

    lo = left_halo.astype(f32)
    hi = right_halo.astype(f32)
    near, far = near_coef, far_coef
    edge = [
        -near * lo[:, 1] - far * lo[:, 0],
        -far * lo[:, 1],
        far * hi[:, 0],
        near * hi[:, 0] + far * hi[:, 1],
    ]
    spots = (0, 1, nx - 2, nx - 1)
    first_end = ends[:, 0] + sum(float(inverse[0, s]) * e for s, e in zip(spots, edge))
    last_end = ends[:, 1] + sum(float(inverse[nx - 1, s]) * e for s, e in zip(spots, edge))
    before_last = lax.ppermute(last_end.astype(bf16), "ax", ups).astype(f32)
    after_first = lax.ppermute(first_end.astype(bf16), "ax", downs).astype(f32)
    corner_first = float(inverse[0, 0])
    corner_last = float(inverse[nx - 1, nx - 1])
    shared = 1.0 - lhs_alpha * lhs_alpha * corner_first * corner_last
    left_value = jnp.where(
        segment > 0, (before_last - lhs_alpha * corner_last * first_end) / shared, 0.0
    )
    next_last = (last_end - lhs_alpha * corner_last * after_first) / shared
    right_value = jnp.where(
        segment < segments - 1, after_first - lhs_alpha * corner_first * next_last, 0.0
    )
    edge[0] = edge[0] - lhs_alpha * left_value
    edge[3] = edge[3] - lhs_alpha * right_value
    edges = jnp.stack(edge, axis=1)

    dy_high, dy_low = split(tables(ny)[1])
    dz_high, dz_low = split(tables(nz)[1])
    dy_both = jnp.asarray(np.concatenate([dy_high, dy_low], axis=1))
    dz_both = jnp.asarray(np.concatenate([dz_high.T, dz_low.T], axis=0))
    upper = jnp.asarray(sweep_coefs(nx)[1].astype(np.float32))

    bx = 8
    steps = nx // bx

    def whole(*shape):
        zeros = (0,) * len(shape)
        return pl.BlockSpec(shape, lambda i: zeros, pipeline_mode=pl.Buffered(1))

    result = pl.pallas_call(
        functools.partial(main_kernel, nx, ny, nz, bx),
        grid=(steps,),
        out_shape=jax.ShapeDtypeStruct((FIELDS, nx, ny, nz), bf16),
        in_specs=[
            pl.BlockSpec(memory_space=pltpu.SMEM),
            whole(FIELDS, nx, ny, nz),
            whole(FIELDS, 4, ny, nz),
            whole(rows, FIELDS * nx),
            whole(1, 2 * nz),
            whole(2 * ny, 1),
            whole(2, nz),
            whole(ny, nz),
            whole(ny, 2 * ny),
            whole(2 * nz, nz),
            pl.BlockSpec((bx, ny, nz), lambda i: (steps - 1 - i, 0, 0)),
            pl.BlockSpec((3, bx, ny, nz), lambda i: (0, steps - 1 - i, 0, 0)),
            pl.BlockSpec((bx, ny, nz), lambda i: (steps - 1 - i, 0, 0)),
            pl.BlockSpec((9, bx, ny, nz), lambda i: (0, steps - 1 - i, 0, 0)),
        ],
        out_specs=pl.BlockSpec((FIELDS, bx, ny, nz), lambda i: (0, steps - 1 - i, 0, 0)),
        scratch_shapes=[
            pltpu.VMEM((FIELDS, nx, ny, nz), f32),
            pltpu.VMEM((FIELDS, nx, 2 * nz), f32),
            pltpu.VMEM((FIELDS, ny, nz), f32),
            pltpu.VMEM((FIELDS, ny, nz), f32),
            pltpu.VMEM((2, 2, FIELDS, ny, nz), f32),
        ],
        compiler_params=pltpu.CompilerParams(vmem_limit_bytes=48 << 20),
        name="flux_and_penalty",
    )(
        upper, adj, edges, recv,
        origin[:, : 2 * nz], origin[:, 2 * nz :].reshape(2 * ny, 1), ymask, zmask,
        dy_both, dz_both, density[0], velocity[:, 0], pressure[0], metrics[:, 0],
    )
    return result[:, None]


def solution(mesh):
    in_specs = (
        P(None, "blk", "ax", None, None),
        P("blk", "ax", None, None),
        P(None, "blk", "ax", None, None),
        P("blk", "ax", None, None),
        P(None, "blk", "ax", None, None),
        P(),
    )
    out_specs = P(None, "blk", "ax", None, None)
    return jax.shard_map(body, mesh=mesh, in_specs=in_specs, out_specs=out_specs, check_vma=False)
```

time: 993 us -> 60.6 us (0.06); the launches traced: 977 us -> 60.2 us
  other arithmetic: 510 us -> 3.91 us
  local copies, waits for them, and re-layouts: 162 us -> 7.23 us
  between operations: 135 us -> 0.27 us
  loops' own time: 124 us -> 0 us
  matrix products: 28.1 us -> 0 us
  Pallas kernels: 0 us -> 25.2 us
    broadcast_in_dim x38 -> x0, other arithmetic: 168 us -> none  [the longest x21 127 us: line_tables(): lax.linalg.tridiagonal_solve(sub_diag, middle, super_diag, jnp.eye(line_c...]
    div x6 -> x0, other arithmetic: 133 us -> none  [the longest x4 79.7 us: line_tables(): lax.linalg.tridiagonal_solve(sub_diag, middle, super_diag, stencil)]
    another operation x2 -> x0, loops' own time: 124 us -> none  [line_tables(): lax.linalg.tridiagonal_solve(sub_diag, middle, super_diag, stencil)]
    sub x6 -> x1, other arithmetic: 101 us -> 0.01 us  [body(): PW - 1 - cell]
    slice x74 -> x5, local copies, waits for them, and re-layouts: 78.6 us -> 0.12 us  [the longest x1 0.07 us: body(): zmask = jnp.where(column == 0, zlive[0][:, None], 0.0)]
    add x3 -> x2, other arithmetic: 36.6 us -> 0.15 us  [the longest x1 0.08 us: body(): zmask = zmask + jnp.where(column == nz - 1, zlive[1][:, None], 0.0)]
    unnamed x6 -> x0, other arithmetic: 36.1 us -> none
    dot_general x4 -> x0, matrix products: 28.1 us -> none  [the longest x1 12 us: body(): lax.dot_general(batch_inverse, stencil_sum.reshape(field_count, local_cel...]
  transfers between devices with their start and end apart: 5 -> 5, of which waited for: 1 -> 2; matrix products, arithmetic and copies ran while one was open for 62% -> 8% of each run, Pallas kernels for 0% -> 7%
where the time goes in v1:
time: 60.6 us; the launch traced here: 60.2 us
  Pallas kernels  25.2 us (42%)
  starting transfers between devices  15.8 us (26%)
  waiting for transfers between devices  7.81 us (13%)
  local copies, waits for them, and re-layouts  7.23 us (12%)
  other arithmetic  3.91 us (6%)
    pallas_call x1, Pallas kernels, body(): pl.pallas_call(functools.partial(main_kernel, nx, ny, nz, bx), grid=(step...  21 us
    unnamed x17, local copies, waits for them, and re-layouts  6.25 us
    ppermute x1, starting transfers between devices, body(): left_halo = lax.ppermute(adj[:, nx - 2:], 'ax', ups)  6.22 us
    ppermute x1, waiting for transfers between devices, body(): after_first = lax.ppermute(first_end.astype(bf16), 'ax', downs).astype(f32)  5.48 us
    all_to_all x1, starting transfers between devices, body(): lax.all_to_all(send.reshape(blk_count, capacity * PW, FIELDS * nx), 'blk'...  4.16 us
    pallas_call x1, Pallas kernels, body(): pl.pallas_call(functools.partial(pack_kernel, nx, ny, nz, derivative[[0,...  4.13 us
    ppermute x1, starting transfers between devices, body(): before_last = lax.ppermute(last_end.astype(bf16), 'ax', ups).astype(f32)  2.87 us
    ppermute x1, waiting for transfers between devices, body(): before_last = lax.ppermute(last_end.astype(bf16), 'ax', ups).astype(f32)  2.32 us
  transfers between devices with their start and end apart: 5, of which 2 were waited for; matrix products, arithmetic and copies ran while one was open for 8% of the time, Pallas kernels for 7%

profile of v1, /device:TPU:0, one launch (start us, length us, event | category | flops | bytes accessed | tf_op | source)
XLA Modules:
  0.0 60.2 jit_solution(15723525107176540618)
XLA Ops:
  0.0 0.0 copy-start.7
  0.0 0.0 copy-start.6
  0.0 3.7 %copy.47 = bf16[5,1,64,64,128]{4,3,0,2,1:T(8,128)(2,1)S(1)} copy(bf16[5,1,64,64,128]{4,3,2,1,0:T(8,128)(2,1)} %param.10) | data formatting | bytes 10485760 | tf_op args[0]
  3.8 1.3 %collective-permute-start.1 = (bf16[5,2,64,128]{3,2,0,1:T(8,128)(2,1)S(1)}, bf16[5,2,64,128]{3,2,0,1:T(8,128)(2,1)}, u32[]{:S(2)}, u32[]{:S(2)}) collective-permute-start(bf16[5,2,64,128]{3,2,0,1:T(8,128)(2,1)S(1)} %get-tuple-element.14), channel_id=1, source_target_pairs={{1,0},{2,1},{3,2},{5,4},{6,5},{7,6},{9,8},{10,9},{11,10},{13,12},{... | collective-permute-start | bytes 491528 | tf_op jit(solution)/shard_map/ppermute | solution.py:236
  5.1 6.2 %collective-permute-start = (bf16[5,2,64,128]{3,2,0,1:T(8,128)(2,1)S(1)}, bf16[5,2,64,128]{3,2,0,1:T(8,128)(2,1)}, u32[]{:S(2)}, u32[]{:S(2)}) collective-permute-start(bf16[5,2,64,128]{3,2,0,1:T(8,128)(2,1)S(1)} %get-tuple-element.13), channel_id=1, source_target_pairs={{0,1},{1,2},{2,3},{4,5},{5,6},{6,7},{8,9},{9,10},{10,11},{12,13},{... | collective-permute-start | bytes 491528 | tf_op jit(solution)/shard_map/ppermute | solution.py:235
  11.3 0.0 copy-done.6
  11.3 0.0 copy-done.7
  11.3 0.3 convert_reduce_fusion
  11.6 0.1 add_add_fusion
  11.7 1.0 %select_reduce_fusion = s32[48]{0:T(128)S(1)} fusion(s32[8,48]{1,0:T(8,128)S(1)} %add_add_fusion, s32[8,48]{1,0:T(8,128)S(1)} %get-tuple-element.18, pred[8,48]{1,0:T(8,128)(4,1)S(1)} %compare_bitcast_fusion), kind=kLoop, calls=%fused_computation.4 | loop fusion | flops 73680 | bytes 3648 | tf_op jit(solution)/shard_map/reduce_sum | solution.py:244
  12.7 0.1 add_select_fusion.1
  12.8 0.1 select_n.73.target_ref
  12.9 0.0 copy-start
  12.9 2.5 %copy-done = bf16[5,1,64,64,128]{4,3,2,1,0:T(8,128)(2,1)S(1)} copy-done((bf16[5,1,64,64,128]{4,3,2,1,0:T(8,128)(2,1)S(1)}, bf16[5,1,64,64,128]{4,3,2,1,0:T(8,128)(2,1)}, u32[]{:S(2)}) %copy-start) | copy-done | bytes 5242904
  15.4 0.0 copy-start.5
  15.4 4.1 %pack_faces.1 = (bf16[384,320]{1,0:T(8,128)(2,1)}, f32[5,2,64,128]{3,2,1,0:T(8,128)S(1)}) custom-call(s32[1,384]{1,0:T(1,128)S(1)} %select_n.73.target_ref, bf16[5,64,64,128]{3,2,1,0:T(8,128)(2,1)S(1)} %bitcast.102), custom_call_target="tpu_custom_call" | custom-call | tf_op jit(solution)/shard_map/pack_faces/pallas_call | solution.py:262
  19.5 4.2 %all-to-all-start = ((bf16[8,48,320]{2,1,0:T(8,128)(2,1)}), bf16[8,48,320]{2,1,0:T(8,128)(2,1)S(1)}, u32[]{:S(2)}, u32[]{:S(2)}) async-start(bf16[8,48,320]{2,1,0:T(8,128)(2,1)} %bitcast.18), calls=%async_computation | async-start | bytes 589824 | tf_op jit(solution)/shard_map/all_to_all | solution.py:285
  23.7 0.1 add_select_fusion
  23.8 0.1 select_n.80
  23.9 0.1 slice_bitcast_fusion.5
  24.0 0.1 copy.39.zsrc_ref
  24.2 0.1 broadcast_in_dim.134
  24.2 0.1 broadcast_in_dim.135
  24.3 0.1 broadcast_in_dim.139
  24.4 0.1 broadcast_in_dim.140
  24.5 0.1 broadcast_in_dim.130
  24.5 0.1 broadcast_in_dim.131
  24.6 0.1 broadcast_in_dim.132.ymask_ref
  24.7 0.1 select_add_fusion.zmask_ref
  24.8 0.0 collective-permute-done.1
  24.8 0.9 %convert_element_type.35 = f32[5,2,64,128]{3,2,0,1:T(8,128)S(1)} convert(bf16[5,2,64,128]{3,2,0,1:T(8,128)(2,1)} %collective-permute-done.1) | non-fusion elementwise | flops 81920 | bytes 491520 | tf_op jit(solution)/shard_map/convert_element_type | solution.py:290
  25.8 0.0 collective-permute-done
  25.8 0.9 %convert_element_type.33 = f32[5,2,64,128]{3,2,0,1:T(8,128)S(1)} convert(bf16[5,2,64,128]{3,2,0,1:T(8,128)(2,1)} %collective-permute-done) | non-fusion elementwise | flops 81920 | bytes 491520 | tf_op jit(solution)/shard_map/convert_element_type | solution.py:289
  26.7 0.1 fusion.19
  26.8 2.9 %collective-permute-start.2 = (bf16[5,64,128]{2,1,0:T(8,128)(2,1)S(1)}, bf16[5,64,128]{2,1,0:T(8,128)(2,1)S(1)}, u32[]{:S(2)}, u32[]{:S(2)}) collective-permute-start(bf16[5,64,128]{2,1,0:T(8,128)(2,1)S(1)} %get-tuple-element.11), channel_id=1, source_target_pairs={{0,1},{1,2},{2,3},{4,5},{5,6},{6,7},{8,9},{9,10},{10,11},{12,13},{... | collective-permute-start | bytes 245768 | tf_op jit(solution)/shard_map/ppermute | solution.py:301
  29.7 2.3 %collective-permute-done.2 = bf16[5,64,128]{2,1,0:T(8,128)(2,1)S(1)} collective-permute-done((bf16[5,64,128]{2,1,0:T(8,128)(2,1)S(1)}, bf16[5,64,128]{2,1,0:T(8,128)(2,1)S(1)}, u32[]{:S(2)}, u32[]{:S(2)}) %collective-permute-start.2) | collective-permute-done | bytes 81952 | tf_op jit(solution)/shard_map/ppermute | solution.py:301
  32.0 0.1 subtract_bitcast_fusion
  32.2 1.3 %collective-permute-start.3 = (bf16[5,64,128]{2,1,0:T(8,128)(2,1)S(1)}, bf16[5,64,128]{2,1,0:T(8,128)(2,1)S(1)}, u32[]{:S(2)}, u32[]{:S(2)}) collective-permute-start(bf16[5,64,128]{2,1,0:T(8,128)(2,1)S(1)} %get-tuple-element.10), channel_id=1, source_target_pairs={{1,0},{2,1},{3,2},{5,4},{6,5},{7,6},{9,8},{10,9},{11,10},{13,12},{... | collective-permute-start | bytes 245768 | tf_op jit(solution)/shard_map/ppermute | solution.py:302
  33.5 5.5 %collective-permute-done.3 = bf16[5,64,128]{2,1,0:T(8,128)(2,1)S(1)} collective-permute-done((bf16[5,64,128]{2,1,0:T(8,128)(2,1)S(1)}, bf16[5,64,128]{2,1,0:T(8,128)(2,1)S(1)}, u32[]{:S(2)}, u32[]{:S(2)}) %collective-permute-start.3) | collective-permute-done | bytes 81952 | tf_op jit(solution)/shard_map/ppermute | solution.py:302
  39.0 0.1 fusion.6
  39.1 0.1 pad_maximum_fusion.edge_ref
  39.1 0.0 all-to-all-done
  39.1 0.0 copy-done.1
  39.1 0.0 copy-done.2
  39.2 0.0 copy-done.3
  39.2 0.0 copy-done.4
  39.2 0.0 copy-done.5
  39.2 21.0 %flux_and_penalty.1 = bf16[5,64,64,128]{3,2,1,0:T(8,128)(2,1)} custom-call(f32[64]{0:T(128)S(1)} %copy-done.5, bf16[5,64,64,128]{3,2,1,0:T(8,128)(2,1)} %bitcast.101, f32[5,4,64,128]{3,2,1,0:T(8,128)S(1)} %pad_maximum_fusion.edge_ref, bf16[384,320]{1,0:T(8,128)(2,1)S(1)} %bitcast.103, s32[1,256]{1,0:T(1,128)S(1)} %slice.98.ysrc_ref, ...), custom_call_target="tpu_custom_call" | custom-call | tf_op jit(solution)/shard_map/flux_and_penalty/pallas_call | solution.py:330
  (20 shorter events, 0.2 us)
Async XLA Ops:
  0.0 11.3 %copy-start.7 = (pred[48,48]{1,0:T(8,128)(4,1)S(1)}, pred[48,48]{1,0:T(8,128)(4,1)}, u32[]{:S(2)}) copy-start(pred[48,48]{1,0:T(8,128)(4,1)} %constant.92) | copy-start | bytes 6916
  0.0 11.3 %copy-start.6 = (s32[3,8,48]{2,1,0:T(8,128)S(1)}, s32[3,8,48]{2,1,0:T(8,128)}, u32[]{:S(2)}) copy-start(s32[3,8,48]{2,1,0:T(8,128)} %param.15) | copy-start | bytes 13828
  3.8 21.0 %collective-permute-start.1 = (bf16[5,2,64,128]{3,2,0,1:T(8,128)(2,1)S(1)}, bf16[5,2,64,128]{3,2,0,1:T(8,128)(2,1)}, u32[]{:S(2)}, u32[]{:S(2)}) collective-permute-start(bf16[5,2,64,128]{3,2,0,1:T(8,128)(2,1)S(1)} %get-tuple-element.14), channel_id=1, source_target_pairs={{1,0},{2,1},{3,2},{5,4},{6,5},{7,6},{9,8},{10,9},{11,10},{13,12},{... | collective-permute-start | bytes 491528 | tf_op jit(solution)/shard_map/ppermute | solution.py:236
  5.1 20.7 %collective-permute-start = (bf16[5,2,64,128]{3,2,0,1:T(8,128)(2,1)S(1)}, bf16[5,2,64,128]{3,2,0,1:T(8,128)(2,1)}, u32[]{:S(2)}, u32[]{:S(2)}) collective-permute-start(bf16[5,2,64,128]{3,2,0,1:T(8,128)(2,1)S(1)} %get-tuple-element.13), channel_id=1, source_target_pairs={{0,1},{1,2},{2,3},{4,5},{5,6},{6,7},{8,9},{9,10},{10,11},{12,13},{... | collective-permute-start | bytes 491528 | tf_op jit(solution)/shard_map/ppermute | solution.py:235
  12.9 2.5 %copy-start = (bf16[5,1,64,64,128]{4,3,2,1,0:T(8,128)(2,1)S(1)}, bf16[5,1,64,64,128]{4,3,2,1,0:T(8,128)(2,1)}, u32[]{:S(2)}) copy-start(bf16[5,1,64,64,128]{4,3,2,1,0:T(8,128)(2,1)} %param.10) | copy-start | bytes 15728644
  15.4 23.8 %copy-start.1 = (bf16[1,64,64,128]{3,2,1,0:T(8,128)(2,1)S(1)}, bf16[1,64,64,128]{3,2,1,0:T(8,128)(2,1)}, u32[]{:S(2)}) copy-start(bf16[1,64,64,128]{3,2,1,0:T(8,128)(2,1)} %param.11) | copy-start | bytes 3145732
  15.4 23.8 %copy-start.2 = (bf16[1,64,64,128]{3,2,1,0:T(8,128)(2,1)S(1)}, bf16[1,64,64,128]{3,2,1,0:T(8,128)(2,1)}, u32[]{:S(2)}) copy-start(bf16[1,64,64,128]{3,2,1,0:T(8,128)(2,1)} %param.13) | copy-start | bytes 3145732
  15.4 23.8 %copy-start.3 = (bf16[256,128]{1,0:T(8,128)(2,1)S(1)}, bf16[256,128]{1,0:T(8,128)(2,1)}, u32[]{:S(2)}) copy-start(bf16[256,128]{1,0:T(8,128)(2,1)} %constant.85.clone.dz_ref) | copy-start | bytes 196612
  15.4 23.8 %copy-start.4 = (bf16[64,128]{1,0:T(8,128)(2,1)S(1)}, bf16[64,128]{1,0:T(8,128)(2,1)}, u32[]{:S(2)}) copy-start(bf16[64,128]{1,0:T(8,128)(2,1)} %constant.84.clone.dy_ref) | copy-start | bytes 49156
  15.4 23.8 %copy-start.5 = (f32[64]{0:T(128)S(1)}, f32[64]{0:T(128)}, u32[]{:S(2)}) copy-start(f32[64]{0:T(128)} %constant.86.clone.upper_ref) | copy-start | bytes 772
  19.5 19.6 %all-to-all-start = ((bf16[8,48,320]{2,1,0:T(8,128)(2,1)}), bf16[8,48,320]{2,1,0:T(8,128)(2,1)S(1)}, u32[]{:S(2)}, u32[]{:S(2)}) async-start(bf16[8,48,320]{2,1,0:T(8,128)(2,1)} %bitcast.18), calls=%async_computation | async-start | bytes 589824 | tf_op jit(solution)/shard_map/all_to_all | solution.py:285
  26.8 5.2 %collective-permute-start.2 = (bf16[5,64,128]{2,1,0:T(8,128)(2,1)S(1)}, bf16[5,64,128]{2,1,0:T(8,128)(2,1)S(1)}, u32[]{:S(2)}, u32[]{:S(2)}) collective-permute-start(bf16[5,64,128]{2,1,0:T(8,128)(2,1)S(1)} %get-tuple-element.11), channel_id=1, source_target_pairs={{0,1},{1,2},{2,3},{4,5},{5,6},{6,7},{8,9},{9,10},{10,11},{12,13},{... | collective-permute-start | bytes 245768 | tf_op jit(solution)/shard_map/ppermute | solution.py:301
  32.2 6.8 %collective-permute-start.3 = (bf16[5,64,128]{2,1,0:T(8,128)(2,1)S(1)}, bf16[5,64,128]{2,1,0:T(8,128)(2,1)S(1)}, u32[]{:S(2)}, u32[]{:S(2)}) collective-permute-start(bf16[5,64,128]{2,1,0:T(8,128)(2,1)S(1)} %get-tuple-element.10), channel_id=1, source_target_pairs={{1,0},{2,1},{3,2},{5,4},{6,5},{7,6},{9,8},{10,9},{11,10},{13,12},{... | collective-permute-start | bytes 245768 | tf_op jit(solution)/shard_map/ppermute | solution.py:302

commit v2 on v1

--- a/solution.py
+++ b/solution.py
@@ -44,7 +44,10 @@
     return weight, upper
 
 
-def pack_kernel(nx, ny, nz, end_rows, target_ref, adj_ref, send_ref, ends_ref, yface, zface):
+def pack_kernel(
+    nx, ny, nz, end_rows, target_ref, adj_ref,
+    send_ref, ends_ref, yown_ref, zown_ref, yface, zface,
+):
     f = pl.program_id(0)
     lane = lax.broadcasted_iota(jnp.int32, (ny, nz), 1)
     first = jnp.zeros((ny, nz), f32)
@@ -61,6 +64,8 @@
     ends_ref[0, 0] = first
     ends_ref[0, 1] = last
     zface[f] = sides
+    zown_ref[0] = sides.astype(bf16)
+    yown_ref[0] = yface[f].astype(bf16)
 
     @pl.when(f == FIELDS - 1)
     def _():
@@ -91,9 +96,167 @@
         send_ref[...] = packed.astype(bf16)
 
 
+def exchange_kernel(
+    nx, blocks, segments, inverse,
+    adj_ref, send_ref, ends_ref, recv_ref, edge_ref,
+    landed, halo, ends, outgoing, beside, patch_send, patch_recv, line_send, line_recv,
+):
+    me = lax.axis_index("blk")
+    seg = lax.axis_index("ax")
+    mesh_ids = pl.DeviceIdType.MESH
+    has_left = seg > 0
+    has_right = seg < segments - 1
+
+    def line_copy(number, source, target, device):
+        return pltpu.make_async_remote_copy(
+            src_ref=source,
+            dst_ref=target,
+            send_sem=line_send.at[number],
+            recv_sem=line_recv.at[number],
+            device_id=(me, device),
+            device_id_type=mesh_ids,
+        )
+
+    halo_right = line_copy(0, adj_ref.at[:, pl.ds(nx - 2, 2)], halo.at[0], seg + 1)
+    halo_left = line_copy(1, adj_ref.at[:, pl.ds(0, 2)], halo.at[1], seg - 1)
+    ends_right = line_copy(2, outgoing.at[1], beside.at[0], seg + 1)
+    ends_left = line_copy(3, outgoing.at[0], beside.at[1], seg - 1)
+
+    def patch_copy(shift):
+        other = lax.rem(me + shift, blocks)
+        return pltpu.make_async_remote_copy(
+            src_ref=send_ref.at[other],
+            dst_ref=landed.at[me],
+            send_sem=patch_send.at[shift],
+            recv_sem=patch_recv.at[shift],
+            device_id=(other, seg),
+            device_id_type=mesh_ids,
+        )
+
+    barrier = pltpu.get_barrier_semaphore()
+    for shift in range(1, blocks):
+        pl.semaphore_signal(
+            barrier, inc=1, device_id=(lax.rem(me + shift, blocks), seg), device_id_type=mesh_ids
+        )
+
+    @pl.when(has_left)
+    def _():
+        pl.semaphore_signal(barrier, inc=1, device_id=(me, seg - 1), device_id_type=mesh_ids)
+
+    @pl.when(has_right)
+    def _():
+        pl.semaphore_signal(barrier, inc=1, device_id=(me, seg + 1), device_id_type=mesh_ids)
+
+    @pl.when(jnp.logical_not(has_left))
+    def _():
+        halo[0] = jnp.zeros_like(halo[0])
+        beside[0] = jnp.zeros_like(beside[0])
+
+    @pl.when(jnp.logical_not(has_right))
+    def _():
+        halo[1] = jnp.zeros_like(halo[1])
+        beside[1] = jnp.zeros_like(beside[1])
+
+    pl.semaphore_wait(
+        barrier, blocks - 1 + has_left.astype(jnp.int32) + has_right.astype(jnp.int32)
+    )
+
+    @pl.when(has_right)
+    def _():
+        halo_right.start()
+
+    @pl.when(has_left)
+    def _():
+        halo_left.start()
+
+    patches = [patch_copy(shift) for shift in range(1, blocks)]
+    for copy in patches:
+        copy.start()
+    recv_ref[me] = send_ref[me]
+
+    @pl.when(has_left)
+    def _():
+        halo_right.wait_recv()
+
+    @pl.when(has_right)
+    def _():
+        halo_left.wait_recv()
+
+    spots = (0, 1, nx - 2, nx - 1)
+
+    def halo_terms(f):
+        lo = [halo[0, f, i].astype(f32) for i in range(2)]
+        hi = [halo[1, f, i].astype(f32) for i in range(2)]
+        return [
+            -near_coef * lo[1] - far_coef * lo[0],
+            -far_coef * lo[1],
+            far_coef * hi[0],
+            near_coef * hi[0] + far_coef * hi[1],
+        ]
+
+    for f in range(FIELDS):
+        terms = halo_terms(f)
+        for side, line in ((0, 0), (1, nx - 1)):
+            value = ends_ref[f, side]
+            for spot, term in zip(spots, terms):
+                value = value + float(inverse[line, spot]) * term
+            ends[side, f] = value
+            outgoing[side, f] = value.astype(bf16)
+
+    @pl.when(has_right)
+    def _():
+        ends_right.start()
+
+    @pl.when(has_left)
+    def _():
+        ends_left.start()
+
+    corner_first = float(inverse[0, 0])
+    corner_last = float(inverse[nx - 1, nx - 1])
+    shared = 1.0 / (1.0 - lhs_alpha * lhs_alpha * corner_first * corner_last)
+
+    @pl.when(has_left)
+    def _():
+        ends_right.wait_recv()
+
+    @pl.when(has_right)
+    def _():
+        ends_left.wait_recv()
+
+    for f in range(FIELDS):
+        terms = halo_terms(f)
+        before_last = beside[0, f].astype(f32)
+        after_first = beside[1, f].astype(f32)
+        left = (before_last - lhs_alpha * corner_last * ends[0, f]) * shared
+        next_last = (ends[1, f] - lhs_alpha * corner_last * after_first) * shared
+        right = after_first - lhs_alpha * corner_first * next_last
+        edge_ref[f, 0] = terms[0] - jnp.where(has_left, lhs_alpha * left, 0.0)
+        edge_ref[f, 1] = terms[1]
+        edge_ref[f, 2] = terms[2]
+        edge_ref[f, 3] = terms[3] - jnp.where(has_right, lhs_alpha * right, 0.0)
+
+    for shift, copy in enumerate(patches, 1):
+        copy.wait_recv()
+        origin = lax.rem(me + blocks - shift, blocks)
+        recv_ref[origin] = landed[origin]
+    for copy in patches:
+        copy.wait_send()
+
+    @pl.when(has_right)
+    def _():
+        halo_right.wait_send()
+        ends_right.wait_send()
+
+    @pl.when(has_left)
+    def _():
+        halo_left.wait_send()
+        ends_left.wait_send()
+
+
 def main_kernel(
     nx, ny, nz, bx,
     upper_ref, adj_ref, edge_ref, recv_ref, ysrc_ref, zsrc_ref, ymask_ref, zmask_ref,
+    yown_ref, zown_ref,
     dy_ref, dz_ref, rho_ref, vel_ref, prs_ref, met_ref,
     out_ref,
     sweep, ypen, zpen, carry, gyz,
@@ -109,9 +272,10 @@
         received = recv_ref[...]
         slots = lax.broadcasted_iota(jnp.int32, (rows, 2 * nz), 0)
         ypick = jnp.where(slots == ysrc_ref[...], 1.0, 0.0).astype(bf16)
-        ypen[...] = lax.dot_general(
+        yother = lax.dot_general(
             received, ypick, (((0,), (0,)), ((), ())), preferred_element_type=f32
         ).reshape(FIELDS, nx, 2 * nz)
+        ypen[...] = ymask_ref[...] * (yother - yown_ref[...].astype(f32))
         slots = lax.broadcasted_iota(jnp.int32, (2 * ny, rows), 1)
         zpick = jnp.where(slots == zsrc_ref[...], 1.0, 0.0).astype(bf16)
         zcells = jnp.dot(zpick, received, preferred_element_type=f32).astype(bf16)
@@ -123,7 +287,8 @@
             both = jnp.concatenate(
                 [zcells[:ny, f * nx : (f + 1) * nx], zcells[ny:, f * nx : (f + 1) * nx]], axis=1
             )
-            zpen[f] = jnp.dot(both, order, preferred_element_type=f32)
+            zother = jnp.dot(both, order, preferred_element_type=f32)
+            zpen[f] = zmask_ref[...] * (zother - zown_ref[f].astype(f32))
 
         def forward(index, state):
             f = index // (ny // part)
@@ -149,6 +314,9 @@
 
     chunk = 16 if ny % 16 == 0 else ny
     unroll = 2
+    row = lax.broadcasted_iota(jnp.int32, (chunk, nz), 0)
+    lane = lax.broadcasted_iota(jnp.int32, (chunk, nz), 1)
+    zedge = (lane == 0) | (lane == nz - 1)
 
     def one(j, slot):
         x = block * bx + j
@@ -193,22 +361,20 @@
                     add(i + 1, k[i] * coupled)
                 dot = k[0] * g[1] + k[1] * g[2] + k[2] * g[3]
                 turned = dot if turned is None else turned + dot
-            add(4, turned / rho)
-            zmask = zmask_ref[at, :]
+            inverse = pl.reciprocal(rho, approx=True)
+            inverse = inverse * (2.0 - rho * inverse)
+            add(4, turned * inverse)
             for f in range(FIELDS):
-                own = adj_ref[f, x, at, :].astype(f32)
-                other = pltpu.roll(zpen[f, at, :], nz - 1 - 2 * x, 1)
-                total = totals[f] + zmask * (other - own)
+                jump = pltpu.roll(zpen[f, at, :], nz - 1 - 2 * x, 1)
+                total = totals[f] + jnp.where(zedge, jump, 0.0)
                 if y0 == 0:
-                    spot = lax.broadcasted_iota(jnp.int32, (chunk, nz), 0) == 0
-                    near_rows = pltpu.roll(ypen[f, group, 0:nz], lax.rem(bx - j, bx), 0)
-                    jump = jnp.concatenate([near_rows] * (chunk // bx), axis=0) - own
-                    total = total + jnp.where(spot, ymask_ref[0:1, :] * jump, 0.0)
+                    jump = pltpu.roll(ypen[f, group, 0:nz], lax.rem(bx - j, bx), 0)
+                    jump = jnp.concatenate([jump] * (chunk // bx), axis=0)
+                    total = total + jnp.where(row == 0, jump, 0.0)
                 if y0 + chunk == ny:
-                    spot = lax.broadcasted_iota(jnp.int32, (chunk, nz), 0) == chunk - 1
-                    near_rows = pltpu.roll(ypen[f, group, nz : 2 * nz], bx - 1 - j, 0)
-                    jump = jnp.concatenate([near_rows] * (chunk // bx), axis=0) - own
-                    total = total + jnp.where(spot, ymask_ref[1:2, :] * jump, 0.0)
+                    jump = pltpu.roll(ypen[f, group, nz : 2 * nz], bx - 1 - j, 0)
+                    jump = jnp.concatenate([jump] * (chunk // bx), axis=0)
+                    total = total + jnp.where(row == chunk - 1, jump, 0.0)
                 out_ref[f, j, at, :] = total.astype(bf16)
 
     def several(i, state):
@@ -225,15 +391,9 @@
     blocks, patches = links.shape[1:]
     blk_count = lax.axis_size("blk")
     segments = lax.axis_size("ax")
-    segment = lax.axis_index("ax")
     me = lax.axis_index("blk")
     capacity = -(-patches // blocks)
     inverse, derivative = tables(nx)
-
-    ups = [(i, i + 1) for i in range(segments - 1)]
-    downs = [(i + 1, i) for i in range(segments - 1)]
-    left_halo = lax.ppermute(adj[:, nx - 2 :], "ax", ups)
-    right_halo = lax.ppermute(adj[:, :2], "ax", downs)
 
     source, face, turn = links[0], links[1], links[2]
     earlier = np.tril(np.ones((patches, patches), bool), -1)[None]
@@ -252,19 +412,20 @@
     live = penalty_weight * jnp.broadcast_to(
         (own_source >= 0).astype(f32), (patches, PW)
     ).reshape(-1)
-    ymask = live[: 2 * nz].reshape(2, nz)
+    ymask = live[: 2 * nz].reshape(1, 2 * nz)
     zlive = live[2 * nz :].reshape(2, ny)
     column = jnp.arange(nz, dtype=jnp.int32)[None, :]
-    zmask = jnp.where(column == 0, zlive[0][:, None], 0.0)
-    zmask = zmask + jnp.where(column == nz - 1, zlive[1][:, None], 0.0)
+    zmask = jnp.where(column % 2 == 1, zlive[0][:, None], zlive[1][:, None])
 
     rows = blk_count * capacity * PW
-    send, ends = pl.pallas_call(
+    send, ends, yown, zown = pl.pallas_call(
         functools.partial(pack_kernel, nx, ny, nz, derivative[[0, nx - 1]]),
         grid=(FIELDS,),
         out_shape=(
             jax.ShapeDtypeStruct((rows, FIELDS * nx), bf16),
             jax.ShapeDtypeStruct((FIELDS, 2, ny, nz), f32),
+            jax.ShapeDtypeStruct((FIELDS, nx, 2 * nz), bf16),
+            jax.ShapeDtypeStruct((FIELDS, ny, nz), bf16),
         ),
         in_specs=[
             pl.BlockSpec((1, 2 * nz + 2 * ny), lambda f: (0, 0)),
@@ -273,46 +434,46 @@
         out_specs=(
             pl.BlockSpec((rows, FIELDS * nx), lambda f: (0, 0)),
             pl.BlockSpec((1, 2, ny, nz), lambda f: (f, 0, 0, 0)),
+            pl.BlockSpec((1, nx, 2 * nz), lambda f: (f, 0, 0)),
+            pl.BlockSpec((1, ny, nz), lambda f: (f, 0, 0)),
         ),
         scratch_shapes=[
             pltpu.VMEM((FIELDS, nx, 2 * nz), f32),
             pltpu.VMEM((FIELDS, ny, nz), f32),
         ],
-        compiler_params=pltpu.CompilerParams(vmem_limit_bytes=32 << 20),
+        compiler_params=pltpu.CompilerParams(vmem_limit_bytes=56 << 20),
         name="pack_faces",
     )(target, adj)
 
-    recv = lax.all_to_all(
-        send.reshape(blk_count, capacity * PW, FIELDS * nx), "blk", 0, 0, tiled=True
-    ).reshape(rows, FIELDS * nx)
-
-    lo = left_halo.astype(f32)
-    hi = right_halo.astype(f32)
-    near, far = near_coef, far_coef
-    edge = [
-        -near * lo[:, 1] - far * lo[:, 0],
-        -far * lo[:, 1],
-        far * hi[:, 0],
-        near * hi[:, 0] + far * hi[:, 1],
-    ]
-    spots = (0, 1, nx - 2, nx - 1)
-    first_end = ends[:, 0] + sum(float(inverse[0, s]) * e for s, e in zip(spots, edge))
-    last_end = ends[:, 1] + sum(float(inverse[nx - 1, s]) * e for s, e in zip(spots, edge))
-    before_last = lax.ppermute(last_end.astype(bf16), "ax", ups).astype(f32)
-    after_first = lax.ppermute(first_end.astype(bf16), "ax", downs).astype(f32)
-    corner_first = float(inverse[0, 0])
-    corner_last = float(inverse[nx - 1, nx - 1])
-    shared = 1.0 - lhs_alpha * lhs_alpha * corner_first * corner_last
-    left_value = jnp.where(
-        segment > 0, (before_last - lhs_alpha * corner_last * first_end) / shared, 0.0
-    )
-    next_last = (last_end - lhs_alpha * corner_last * after_first) / shared
-    right_value = jnp.where(
-        segment < segments - 1, after_first - lhs_alpha * corner_first * next_last, 0.0
-    )
-    edge[0] = edge[0] - lhs_alpha * left_value
-    edge[3] = edge[3] - lhs_alpha * right_value
-    edges = jnp.stack(edge, axis=1)
+    slab = (capacity * PW, FIELDS * nx)
+    layers = (FIELDS, 2, ny, nz)
+    level = (FIELDS, ny, nz)
+    vmem = pl.BlockSpec(memory_space=pltpu.VMEM)
+    recv, edges = pl.pallas_call(
+        functools.partial(exchange_kernel, nx, blk_count, segments, inverse),
+        out_shape=(
+            jax.ShapeDtypeStruct((blk_count,) + slab, bf16),
+            jax.ShapeDtypeStruct((FIELDS, 4, ny, nz), f32),
+        ),
+        in_specs=[pl.BlockSpec(memory_space=pl.ANY), vmem, vmem],
+        out_specs=(vmem, vmem),
+        scratch_shapes=[
+            pltpu.VMEM((blk_count,) + slab, bf16),
+            pltpu.VMEM((2,) + layers, bf16),
+            pltpu.VMEM((2,) + level, f32),
+            pltpu.VMEM((2,) + level, bf16),
+            pltpu.VMEM((2,) + level, bf16),
+            pltpu.SemaphoreType.DMA((blk_count,)),
+            pltpu.SemaphoreType.DMA((blk_count,)),
+            pltpu.SemaphoreType.DMA((4,)),
+            pltpu.SemaphoreType.DMA((4,)),
+        ],
+        compiler_params=pltpu.CompilerParams(
+            collective_id=0, has_side_effects=True, vmem_limit_bytes=32 << 20
+        ),
+        name="exchange",
+    )(adj, send.reshape((blk_count,) + slab), ends)
+    recv = recv.reshape(rows, FIELDS * nx)
 
     dy_high, dy_low = split(tables(ny)[1])
     dz_high, dz_low = split(tables(nz)[1])
@@ -338,8 +499,10 @@
             whole(rows, FIELDS * nx),
             whole(1, 2 * nz),
             whole(2 * ny, 1),
-            whole(2, nz),
+            whole(1, 2 * nz),
             whole(ny, nz),
+            whole(FIELDS, nx, 2 * nz),
+            whole(FIELDS, ny, nz),
             whole(ny, 2 * ny),
             whole(2 * nz, nz),
             pl.BlockSpec((bx, ny, nz), lambda i: (steps - 1 - i, 0, 0)),
@@ -360,7 +523,7 @@
     )(
         upper, adj, edges, recv,
         origin[:, : 2 * nz], origin[:, 2 * nz :].reshape(2 * ny, 1), ymask, zmask,
-        dy_both, dz_both, density[0], velocity[:, 0], pressure[0], metrics[:, 0],
+        yown, zown, dy_both, dz_both, density[0], velocity[:, 0], pressure[0], metrics[:, 0],
     )
     return result[:, None]
 

time: 60.6 us -> 50.8 us (0.84)
  Pallas kernels: 25.2 us -> 43.1 us
  starting transfers between devices: 15.8 us -> 0 us
  waiting for transfers between devices: 7.81 us -> 0 us
  local copies, waits for them, and re-layouts: 7.23 us -> 4.12 us
  other arithmetic: 3.91 us -> 3.01 us
    pallas_call x0 -> x1, Pallas kernels: none -> 14.6 us  [body(): pl.pallas_call(functools.partial(exchange_kernel, nx, blk_count, segments...]
    ppermute x4 -> x0, starting transfers between devices: 11.7 us -> none  [the longest x1 6.22 us: body(): left_halo = lax.ppermute(adj[:, nx - 2:], 'ax', ups)]
    ppermute x4 -> x0, waiting for transfers between devices: 7.81 us -> none  [the longest x1 5.48 us: body(): after_first = lax.ppermute(first_end.astype(bf16), 'ax', downs).astype(f32)]
    unnamed x17 -> x20, local copies, waits for them, and re-layouts: 6.25 us -> 1.97 us
    all_to_all x1 -> x0, starting transfers between devices: 4.16 us -> none  [body(): lax.all_to_all(send.reshape(blk_count, capacity * PW, FIELDS * nx), 'blk'...]
    pallas_call x1, Pallas kernels: 4.13 us -> 7.7 us  [body(): pl.pallas_call(functools.partial(pack_kernel, nx, ny, nz, derivative[[0,...]
    convert_element_type x3 -> x0, other arithmetic: 1.98 us -> none  [the longest x1 0.94 us: body(): lo = left_halo.astype(f32)]
    slice x1, local copies, waits for them, and re-layouts: 0.01 us -> 0.72 us  [body(): source, face, turn = (links[0], links[1], links[2])]
  transfers between devices with their start and end apart: 5 -> 0, of which waited for: 2 -> 0; matrix products, arithmetic and copies ran while one was open for 8% -> 0% of each run, Pallas kernels for 7% -> 0%
where the time goes in v2:
time: 50.8 us; the launch traced here: 50.4 us
  Pallas kernels  43.1 us (85%)
  local copies, waits for them, and re-layouts  4.12 us (8%)
  other arithmetic  3.01 us (6%)
    pallas_call x1, Pallas kernels, body(): pl.pallas_call(functools.partial(main_kernel, nx, ny, nz, bx), grid=(step...  20.8 us
    pallas_call x1, Pallas kernels, body(): pl.pallas_call(functools.partial(exchange_kernel, nx, blk_count, segments...  14.6 us
    pallas_call x1, Pallas kernels, body(): pl.pallas_call(functools.partial(pack_kernel, nx, ny, nz, derivative[[0,...  7.7 us
    unnamed x20, local copies, waits for them, and re-layouts  1.97 us

profile of v2, /device:TPU:0, one launch (start us, length us, event | category | flops | bytes accessed | tf_op | source)
XLA Modules:
  0.0 50.4 jit_solution(11965687101531574827)
XLA Ops:
  0.0 0.7 %compare_bitcast_fusion = pred[8,48]{1,0:T(8,128)(4,1)S(1)} fusion(s32[]{:T(128)S(6)} %axis_index.15, s32[3,8,48]{2,1,0:T(8,128)} %param.15), kind=kLoop, calls=%fused_computation.9 | loop fusion | flops 384 | bytes 1924 | tf_op jit(solution)/shard_map/and | solution.py:403
  0.7 0.7 %fusion.5 = (s32[1,8,48]{2,1,0:T(8,128)S(1)}, s32[8,48]{1,0:T(8,128)S(1)}, s32[1,8,48]{2,1,0:T(8,128)S(1)}, s32[8,48]{1,0:T(8,128)S(1)}) fusion(s32[3,8,48]{2,1,0:T(8,128)} %param.15), kind=kLoop, calls=%fused_computation.30 | loop fusion | bytes 10752 | tf_op jit(solution)/shard_map/slice | solution.py:398
  1.5 0.1 slice_bitcast_fusion.3
  1.5 0.1 broadcast_in_dim.115
  1.6 0.1 broadcast_in_dim.116
  1.7 1.0 %convert_reduce_fusion = s32[8,48]{1,0:T(8,128)S(1)} fusion(s32[8,48]{1,0:T(8,128)S(1)} %get-tuple-element.18, pred[48,48]{1,0:T(8,128)(4,1)} %constant.65), kind=kLoop, calls=%fused_computation.1 | loop fusion | flops 73344 | bytes 5376 | tf_op jit(solution)/shard_map/reduce_sum | solution.py:401
  2.7 0.1 add_add_fusion
  2.8 0.9 %select_reduce_fusion = s32[48]{0:T(128)S(1)} fusion(s32[8,48]{1,0:T(8,128)S(1)} %add_add_fusion, s32[8,48]{1,0:T(8,128)S(1)} %get-tuple-element.20, pred[8,48]{1,0:T(8,128)(4,1)S(1)} %compare_bitcast_fusion), kind=kLoop, calls=%fused_computation | loop fusion | flops 73680 | bytes 3648 | tf_op jit(solution)/shard_map/reduce_sum | solution.py:404
  3.8 0.1 broadcast_in_dim.118
  3.8 0.1 broadcast_in_dim.119
  3.9 0.1 broadcast_in_dim.113
  4.0 0.1 reshape.246.ymask_ref
  4.1 0.1 add_select_fusion
  4.2 0.1 select_n.71
  4.3 0.1 add_select_fusion.1
  4.4 0.7 %select_n.67.target_ref = s32[1,384]{1,0:T(1,128)} reshape(s32[48,8]{1,0:T(8,128)S(1)} %add_select_fusion.1) | data formatting | bytes 3072 | tf_op jit(solution)/shard_map/jit(_where)/select_n | solution.py:406
  5.0 0.0 copy-start.8
  5.0 0.1 broadcast_select_fusion.zmask_ref
  5.1 0.0 copy-start.7
  5.1 0.0 copy-start.9
  5.1 0.1 copy.15.zsrc_ref
  5.3 0.0 copy-start
  5.3 0.0 copy-start.1
  5.3 0.0 copy-start.2
  5.3 7.7 %pack_faces.1 = (bf16[384,320]{1,0:T(8,128)(2,1)}, f32[5,2,64,128]{3,2,1,0:T(8,128)}, bf16[5,64,256]{2,1,0:T(8,128)(2,1)}, bf16[5,64,128]{2,1,0:T(8,128)(2,1)}) custom-call(s32[1,384]{1,0:T(1,128)} %select_n.67.target_ref, bf16[5,64,64,128]{3,2,1,0:T(8,128)(2,1)} %bitcast.36), custom_call_target="tpu_custom_call" | custom-call | tf_op jit(solution)/shard_map/pack_faces/pallas_call | solution.py:421
  13.0 0.0 copy-done
  13.0 0.0 copy-start.3
  13.0 1.0 %copy-done.3 = f32[5,2,64,128]{3,2,1,0:T(8,128)S(1)} copy-done((f32[5,2,64,128]{3,2,1,0:T(8,128)S(1)}, f32[5,2,64,128]{3,2,1,0:T(8,128)}, u32[]{:S(2)}) %copy-start.3) | copy-done | bytes 327704
  14.0 0.0 copy-start.4
  14.0 1.0 %copy-done.4 = bf16[384,320]{1,0:T(8,128)(2,1)S(1)} copy-done((bf16[384,320]{1,0:T(8,128)(2,1)S(1)}, bf16[384,320]{1,0:T(8,128)(2,1)}, u32[]{:S(2)}) %copy-start.4) | copy-done | bytes 245784
  14.9 0.0 copy-start.5
  14.9 0.0 copy-start.6
  14.9 14.6 %exchange.1 = (bf16[8,48,320]{2,1,0:T(8,128)(2,1)S(1)}, f32[5,4,64,128]{3,2,1,0:T(8,128)S(1)}) custom-call(bf16[5,64,64,128]{3,2,1,0:T(8,128)(2,1)S(1)} %bitcast.38, bf16[8,48,320]{2,1,0:T(8,128)(2,1)S(1)} %bitcast.41, f32[5,2,64,128]{3,2,1,0:T(8,128)S(1)} %copy-done.3), custom_call_target="tpu_custom_call" | custom-call | tf_op jit(solution)/shard_map/exchange/pallas_call | solution.py:452
  29.5 0.0 copy-done.8
  29.5 0.0 copy-done.7
  29.5 0.0 copy-done.9
  29.5 0.0 copy-done.1
  29.5 0.0 copy-done.2
  29.5 0.0 copy-done.5
  29.6 0.0 copy-done.6
  29.6 20.8 %flux_and_penalty.1 = bf16[5,64,64,128]{3,2,1,0:T(8,128)(2,1)} custom-call(f32[64]{0:T(128)S(1)} %copy-done.9, bf16[5,64,64,128]{3,2,1,0:T(8,128)(2,1)} %bitcast.37, f32[5,4,64,128]{3,2,1,0:T(8,128)S(1)} %get-tuple-element.13.edge_ref, bf16[384,320]{1,0:T(8,128)(2,1)S(1)} %bitcast.42, s32[1,256]{1,0:T(1,128)S(1)} %slice.59.ysrc_ref, ...), custom_call_target="tpu_custom_call" | custom-call | tf_op jit(solution)/shard_map/flux_and_penalty/pallas_call | solution.py:491
  (11 shorter events, 0.1 us)
Async XLA Ops:
  5.0 24.5 %copy-start.8 = (bf16[64,128]{1,0:T(8,128)(2,1)S(1)}, bf16[64,128]{1,0:T(8,128)(2,1)}, u32[]{:S(2)}) copy-start(bf16[64,128]{1,0:T(8,128)(2,1)} %constant.57.clone.dy_ref) | copy-start | bytes 49156
  5.1 24.4 %copy-start.7 = (bf16[256,128]{1,0:T(8,128)(2,1)S(1)}, bf16[256,128]{1,0:T(8,128)(2,1)}, u32[]{:S(2)}) copy-start(bf16[256,128]{1,0:T(8,128)(2,1)} %constant.58.clone.dz_ref) | copy-start | bytes 196612
  5.1 24.4 %copy-start.9 = (f32[64]{0:T(128)S(1)}, f32[64]{0:T(128)}, u32[]{:S(2)}) copy-start(f32[64]{0:T(128)} %constant.59.clone.upper_ref) | copy-start | bytes 772
  5.3 7.7 %copy-start = (bf16[5,1,64,64,128]{4,3,2,1,0:T(8,128)(2,1)S(1)}, bf16[5,1,64,64,128]{4,3,2,1,0:T(8,128)(2,1)}, u32[]{:S(2)}) copy-start(bf16[5,1,64,64,128]{4,3,2,1,0:T(8,128)(2,1)} %param.10) | copy-start | bytes 15728644
  5.3 24.3 %copy-start.1 = (bf16[1,64,64,128]{3,2,1,0:T(8,128)(2,1)S(1)}, bf16[1,64,64,128]{3,2,1,0:T(8,128)(2,1)}, u32[]{:S(2)}) copy-start(bf16[1,64,64,128]{3,2,1,0:T(8,128)(2,1)} %param.11) | copy-start | bytes 3145732
  5.3 24.3 %copy-start.2 = (bf16[1,64,64,128]{3,2,1,0:T(8,128)(2,1)S(1)}, bf16[1,64,64,128]{3,2,1,0:T(8,128)(2,1)}, u32[]{:S(2)}) copy-start(bf16[1,64,64,128]{3,2,1,0:T(8,128)(2,1)} %param.13) | copy-start | bytes 3145732
  13.0 1.0 %copy-start.3 = (f32[5,2,64,128]{3,2,1,0:T(8,128)S(1)}, f32[5,2,64,128]{3,2,1,0:T(8,128)}, u32[]{:S(2)}) copy-start(f32[5,2,64,128]{3,2,1,0:T(8,128)} %get-tuple-element.12.ends_ref) | copy-start | bytes 983044
  14.0 1.0 %copy-start.4 = (bf16[384,320]{1,0:T(8,128)(2,1)S(1)}, bf16[384,320]{1,0:T(8,128)(2,1)}, u32[]{:S(2)}) copy-start(bf16[384,320]{1,0:T(8,128)(2,1)} %get-tuple-element.11) | copy-start | bytes 737284
  14.9 14.6 %copy-start.5 = (bf16[5,64,256]{2,1,0:T(8,128)(2,1)S(1)}, bf16[5,64,256]{2,1,0:T(8,128)(2,1)}, u32[]{:S(2)}) copy-start(bf16[5,64,256]{2,1,0:T(8,128)(2,1)} %get-tuple-element.15.yown_ref) | copy-start | bytes 491524
  14.9 14.6 %copy-start.6 = (bf16[5,64,128]{2,1,0:T(8,128)(2,1)S(1)}, bf16[5,64,128]{2,1,0:T(8,128)(2,1)}, u32[]{:S(2)}) copy-start(bf16[5,64,128]{2,1,0:T(8,128)(2,1)} %get-tuple-element.16.zown_ref) | copy-start | bytes 245764

commit v3 on v2

--- a/solution.py
+++ b/solution.py
@@ -44,63 +44,18 @@
     return weight, upper
 
 
-def pack_kernel(
-    nx, ny, nz, end_rows, target_ref, adj_ref,
-    send_ref, ends_ref, yown_ref, zown_ref, yface, zface,
+def exchange_kernel(
+    nx, ny, nz, blocks, segments, inverse, end_rows,
+    target_ref, adj_ref, recv_ref, edge_ref, yown_ref, zown_ref,
+    fields, send_ref, yface, zface,
+    landed, halo, ends, outgoing, beside,
+    load_sem, patch_send, patch_recv, line_send, line_recv,
 ):
-    f = pl.program_id(0)
-    lane = lax.broadcasted_iota(jnp.int32, (ny, nz), 1)
-    first = jnp.zeros((ny, nz), f32)
-    last = jnp.zeros((ny, nz), f32)
-    sides = jnp.zeros((ny, nz), f32)
-    for x in range(nx):
-        slab = adj_ref[0, x].astype(f32)
-        first = first + float(end_rows[0, x]) * slab
-        last = last + float(end_rows[1, x]) * slab
-        yface[f, x : x + 1, 0:nz] = slab[0:1]
-        yface[f, x : x + 1, nz : 2 * nz] = slab[ny - 1 :]
-        turned = pltpu.roll(slab, 2 * x + 1, 1)
-        sides = jnp.where(lane // 2 == x, turned, sides)
-    ends_ref[0, 0] = first
-    ends_ref[0, 1] = last
-    zface[f] = sides
-    zown_ref[0] = sides.astype(bf16)
-    yown_ref[0] = yface[f].astype(bf16)
-
-    @pl.when(f == FIELDS - 1)
-    def _():
-        row = lax.broadcasted_iota(jnp.int32, (nz, 2 * nx), 0)
-        col = lax.broadcasted_iota(jnp.int32, (nz, 2 * nx), 1)
-        wanted = jnp.where(col < nx, 2 * col + 1, 2 * (col - nx))
-        order = jnp.where(row == wanted, 1.0, 0.0).astype(bf16)
-        low, high = [], []
-        for g in range(FIELDS):
-            sorted_side = jnp.dot(
-                zface[g].astype(bf16), order, preferred_element_type=f32
-            )
-            low.append(sorted_side[:, :nx])
-            high.append(sorted_side[:, nx:])
-        cells = jnp.concatenate(
-            [jnp.concatenate(low, axis=1), jnp.concatenate(high, axis=1)], axis=0
-        ).astype(bf16)
-        rows = send_ref.shape[0]
-        slots = lax.broadcasted_iota(jnp.int32, (rows, 2 * nz + 2 * ny), 0)
-        chosen = jnp.where(slots == target_ref[...], 1.0, 0.0).astype(bf16)
-        packed = lax.dot_general(
-            chosen[:, : 2 * nz],
-            yface[...].reshape(FIELDS * nx, 2 * nz).astype(bf16),
-            (((1,), (1,)), ((), ())),
-            preferred_element_type=f32,
-        )
-        packed = packed + jnp.dot(chosen[:, 2 * nz :], cells, preferred_element_type=f32)
-        send_ref[...] = packed.astype(bf16)
-
-
-def exchange_kernel(
-    nx, blocks, segments, inverse,
-    adj_ref, send_ref, ends_ref, recv_ref, edge_ref,
-    landed, halo, ends, outgoing, beside, patch_send, patch_recv, line_send, line_recv,
-):
+    def load(f):
+        return pltpu.make_async_copy(adj_ref.at[f], fields.at[f], load_sem.at[f])
+
+    for f in range(FIELDS):
+        load(f).start()
     me = lax.axis_index("blk")
     seg = lax.axis_index("ax")
     mesh_ids = pl.DeviceIdType.MESH
@@ -169,10 +124,27 @@
     def _():
         halo_left.start()
 
-    patches = [patch_copy(shift) for shift in range(1, blocks)]
-    for copy in patches:
-        copy.start()
-    recv_ref[me] = send_ref[me]
+    lane = lax.broadcasted_iota(jnp.int32, (ny, nz), 1)
+
+    def read_field(f, state):
+        load(f).wait()
+        first = jnp.zeros((ny, nz), f32)
+        last = jnp.zeros((ny, nz), f32)
+        sides = jnp.zeros((ny, nz), f32)
+        for x in range(nx):
+            slab = fields[f, x].astype(f32)
+            first = first + float(end_rows[0, x]) * slab
+            last = last + float(end_rows[1, x]) * slab
+            yface[f, x : x + 1, 0:nz] = slab[0:1]
+            yface[f, x : x + 1, nz : 2 * nz] = slab[ny - 1 :]
+            turned = pltpu.roll(slab, 2 * x + 1, 1)
+            sides = jnp.where(lane // 2 == x, turned, sides)
+        ends[0, f] = first
+        ends[1, f] = last
+        zface[f] = sides.astype(bf16)
+        return state
+
+    lax.fori_loop(0, FIELDS, read_field, 0)
 
     @pl.when(has_left)
     def _():
@@ -197,7 +169,7 @@
     for f in range(FIELDS):
         terms = halo_terms(f)
         for side, line in ((0, 0), (1, nx - 1)):
-            value = ends_ref[f, side]
+            value = ends[side, f]
             for spot, term in zip(spots, terms):
                 value = value + float(inverse[line, spot]) * term
             ends[side, f] = value
@@ -210,6 +182,38 @@
     @pl.when(has_left)
     def _():
         ends_left.start()
+
+    row = lax.broadcasted_iota(jnp.int32, (nz, 2 * nx), 0)
+    col = lax.broadcasted_iota(jnp.int32, (nz, 2 * nx), 1)
+    wanted = jnp.where(col < nx, 2 * col + 1, 2 * (col - nx))
+    order = jnp.where(row == wanted, 1.0, 0.0).astype(bf16)
+    low, high = [], []
+    for f in range(FIELDS):
+        sorted_side = jnp.dot(zface[f], order, preferred_element_type=f32)
+        low.append(sorted_side[:, :nx])
+        high.append(sorted_side[:, nx:])
+    cells = jnp.concatenate(
+        [jnp.concatenate(low, axis=1), jnp.concatenate(high, axis=1)], axis=0
+    ).astype(bf16)
+    own_rows = yface[...].astype(bf16)
+    rows = blocks * send_ref.shape[1]
+    slots = lax.broadcasted_iota(jnp.int32, (rows, 2 * nz + 2 * ny), 0)
+    chosen = jnp.where(slots == target_ref[...], 1.0, 0.0).astype(bf16)
+    packed = lax.dot_general(
+        chosen[:, : 2 * nz],
+        own_rows.reshape(FIELDS * nx, 2 * nz),
+        (((1,), (1,)), ((), ())),
+        preferred_element_type=f32,
+    )
+    packed = packed + jnp.dot(chosen[:, 2 * nz :], cells, preferred_element_type=f32)
+    send_ref[...] = packed.astype(bf16).reshape(send_ref.shape)
+
+    patches = [patch_copy(shift) for shift in range(1, blocks)]
+    for copy in patches:
+        copy.start()
+    recv_ref[me] = send_ref[me]
+    yown_ref[...] = own_rows
+    zown_ref[...] = zface[...]
 
     corner_first = float(inverse[0, 0])
     corner_last = float(inverse[nx - 1, nx - 1])
@@ -255,11 +259,11 @@
 
 def main_kernel(
     nx, ny, nz, bx,
-    upper_ref, adj_ref, edge_ref, recv_ref, ysrc_ref, zsrc_ref, ymask_ref, zmask_ref,
+    upper_ref, adj_hbm, edge_ref, recv_ref, ysrc_ref, zsrc_ref, ymask_ref, zmask_ref,
     yown_ref, zown_ref,
     dy_ref, dz_ref, rho_ref, vel_ref, prs_ref, met_ref,
     out_ref,
-    sweep, ypen, zpen, carry, gyz,
+    adj_ref, load_sem, sweep, ypen, zpen, carry, gyz,
 ):
     step = pl.program_id(0)
     block = pl.num_programs(0) - 1 - step
@@ -268,6 +272,17 @@
 
     @pl.when(step == 0)
     def _():
+        half = nx // 2
+
+        def load(f, h):
+            at = pl.ds(h * half, half)
+            return pltpu.make_async_copy(
+                adj_hbm.at[f, at], adj_ref.at[f, at], load_sem.at[2 * f + h]
+            )
+
+        for f in range(FIELDS):
+            for h in range(2):
+                load(f, h).start()
         rows = recv_ref.shape[0]
         received = recv_ref[...]
         slots = lax.broadcasted_iota(jnp.int32, (rows, 2 * nz), 0)
@@ -293,6 +308,12 @@
         def forward(index, state):
             f = index // (ny // part)
             at = pl.ds(pl.multiple_of((index % (ny // part)) * part, part), part)
+
+            @pl.when(index % (ny // part) == 0)
+            def _():
+                load(f, 0).wait()
+                load(f, 1).wait()
+
             zero = jnp.zeros((part, nz), f32)
             window = [zero, zero, adj_ref[f, 0, at, :].astype(f32), adj_ref[f, 1, at, :].astype(f32)]
             before = zero
@@ -418,61 +439,43 @@
     zmask = jnp.where(column % 2 == 1, zlive[0][:, None], zlive[1][:, None])
 
     rows = blk_count * capacity * PW
-    send, ends, yown, zown = pl.pallas_call(
-        functools.partial(pack_kernel, nx, ny, nz, derivative[[0, nx - 1]]),
-        grid=(FIELDS,),
-        out_shape=(
-            jax.ShapeDtypeStruct((rows, FIELDS * nx), bf16),
-            jax.ShapeDtypeStruct((FIELDS, 2, ny, nz), f32),
-            jax.ShapeDtypeStruct((FIELDS, nx, 2 * nz), bf16),
-            jax.ShapeDtypeStruct((FIELDS, ny, nz), bf16),
-        ),
-        in_specs=[
-            pl.BlockSpec((1, 2 * nz + 2 * ny), lambda f: (0, 0)),
-            pl.BlockSpec((1, nx, ny, nz), lambda f: (f, 0, 0, 0)),
-        ],
-        out_specs=(
-            pl.BlockSpec((rows, FIELDS * nx), lambda f: (0, 0)),
-            pl.BlockSpec((1, 2, ny, nz), lambda f: (f, 0, 0, 0)),
-            pl.BlockSpec((1, nx, 2 * nz), lambda f: (f, 0, 0)),
-            pl.BlockSpec((1, ny, nz), lambda f: (f, 0, 0)),
-        ),
-        scratch_shapes=[
-            pltpu.VMEM((FIELDS, nx, 2 * nz), f32),
-            pltpu.VMEM((FIELDS, ny, nz), f32),
-        ],
-        compiler_params=pltpu.CompilerParams(vmem_limit_bytes=56 << 20),
-        name="pack_faces",
-    )(target, adj)
-
     slab = (capacity * PW, FIELDS * nx)
     layers = (FIELDS, 2, ny, nz)
     level = (FIELDS, ny, nz)
     vmem = pl.BlockSpec(memory_space=pltpu.VMEM)
-    recv, edges = pl.pallas_call(
-        functools.partial(exchange_kernel, nx, blk_count, segments, inverse),
+    recv, edges, yown, zown = pl.pallas_call(
+        functools.partial(
+            exchange_kernel, nx, ny, nz, blk_count, segments, inverse, derivative[[0, nx - 1]]
+        ),
         out_shape=(
             jax.ShapeDtypeStruct((blk_count,) + slab, bf16),
             jax.ShapeDtypeStruct((FIELDS, 4, ny, nz), f32),
+            jax.ShapeDtypeStruct((FIELDS, nx, 2 * nz), bf16),
+            jax.ShapeDtypeStruct((FIELDS, ny, nz), bf16),
         ),
-        in_specs=[pl.BlockSpec(memory_space=pl.ANY), vmem, vmem],
-        out_specs=(vmem, vmem),
+        in_specs=[vmem, pl.BlockSpec(memory_space=pl.ANY)],
+        out_specs=(vmem, vmem, vmem, vmem),
         scratch_shapes=[
+            pltpu.VMEM((FIELDS, nx, ny, nz), bf16),
+            pltpu.VMEM((blk_count,) + slab, bf16),
+            pltpu.VMEM((FIELDS, nx, 2 * nz), f32),
+            pltpu.VMEM(level, bf16),
             pltpu.VMEM((blk_count,) + slab, bf16),
             pltpu.VMEM((2,) + layers, bf16),
             pltpu.VMEM((2,) + level, f32),
             pltpu.VMEM((2,) + level, bf16),
             pltpu.VMEM((2,) + level, bf16),
+            pltpu.SemaphoreType.DMA((FIELDS,)),
             pltpu.SemaphoreType.DMA((blk_count,)),
             pltpu.SemaphoreType.DMA((blk_count,)),
             pltpu.SemaphoreType.DMA((4,)),
             pltpu.SemaphoreType.DMA((4,)),
         ],
         compiler_params=pltpu.CompilerParams(
-            collective_id=0, has_side_effects=True, vmem_limit_bytes=32 << 20
+            collective_id=0, has_side_effects=True, vmem_limit_bytes=48 << 20
         ),
         name="exchange",
-    )(adj, send.reshape((blk_count,) + slab), ends)
+    )(target, adj)
     recv = recv.reshape(rows, FIELDS * nx)
 
     dy_high, dy_low = split(tables(ny)[1])
@@ -494,7 +497,7 @@
         out_shape=jax.ShapeDtypeStruct((FIELDS, nx, ny, nz), bf16),
         in_specs=[
             pl.BlockSpec(memory_space=pltpu.SMEM),
-            whole(FIELDS, nx, ny, nz),
+            pl.BlockSpec(memory_space=pl.ANY),
             whole(FIELDS, 4, ny, nz),
             whole(rows, FIELDS * nx),
             whole(1, 2 * nz),
@@ -512,6 +515,8 @@
         ],
         out_specs=pl.BlockSpec((FIELDS, bx, ny, nz), lambda i: (0, steps - 1 - i, 0, 0)),
         scratch_shapes=[
+            pltpu.VMEM((FIELDS, nx, ny, nz), bf16),
+            pltpu.SemaphoreType.DMA((2 * FIELDS,)),
             pltpu.VMEM((FIELDS, nx, ny, nz), f32),
             pltpu.VMEM((FIELDS, nx, 2 * nz), f32),
             pltpu.VMEM((FIELDS, ny, nz), f32),

time: 50.8 us -> 40.3 us (0.79)
  Pallas kernels: 43.1 us -> 35.1 us
  local copies, waits for them, and re-layouts: 4.12 us -> 1.59 us
    pallas_call x2 -> x1, Pallas kernels: 22.2 us -> 15 us  [body(): pl.pallas_call(functools.partial(exchange_kernel, nx, ny, nz, blk_count,...]
    unnamed x20 -> x10, local copies, waits for them, and re-layouts: 1.97 us -> 0.02 us
    pallas_call x1, Pallas kernels: 20.8 us -> 20.1 us  [body(): pl.pallas_call(functools.partial(main_kernel, nx, ny, nz, bx), grid=(step...]
    select_n x1, local copies, waits for them, and re-layouts: 0.67 us -> 0.1 us  [body(): jnp.where(slot_of[:, None] >= 0, slot_of[:, None] * PW + cell, -1)]
where the time goes in v3:
time: 40.3 us; the launch traced here: 40 us
  Pallas kernels  35.1 us (87%)
  other arithmetic  3.17 us (8%)
  local copies, waits for them, and re-layouts  1.59 us (4%)
    pallas_call x1, Pallas kernels, body(): pl.pallas_call(functools.partial(main_kernel, nx, ny, nz, bx), grid=(step...  20.1 us
    pallas_call x1, Pallas kernels, body(): pl.pallas_call(functools.partial(exchange_kernel, nx, ny, nz, blk_count,...  15 us
    reduce_sum x1, other arithmetic, body(): slot = jnp.sum(same.astype(jnp.int32), axis=2)  1 us
    reduce_sum x1, other arithmetic, body(): slot_of = jnp.sum(jnp.where(mine, place[None] + 1, 0), axis=(1, 2)) - 1  0.94 us
    and x1, other arithmetic, body(): (source == me)[None]  0.84 us

profile of v3, /device:TPU:0, one launch (start us, length us, event | category | flops | bytes accessed | tf_op | source)
XLA Modules:
  0.0 40.0 jit_solution(12395214553855809782)
XLA Ops:
  0.0 0.0 copy-start.4
  0.0 0.0 copy-start.2
  0.0 0.0 copy-start.3
  0.0 0.0 copy-start.1
  0.0 0.0 copy-start
  0.0 0.8 %compare_bitcast_fusion = pred[8,48]{1,0:T(8,128)(4,1)S(1)} fusion(s32[]{:T(128)S(6)} %axis_index.15, s32[3,8,48]{2,1,0:T(8,128)} %param.15), kind=kLoop, calls=%fused_computation.9 | loop fusion | flops 384 | bytes 1924 | tf_op jit(solution)/shard_map/and | solution.py:424
  0.9 0.7 %fusion.5 = (s32[1,8,48]{2,1,0:T(8,128)S(1)}, s32[8,48]{1,0:T(8,128)S(1)}, s32[1,8,48]{2,1,0:T(8,128)S(1)}, s32[8,48]{1,0:T(8,128)S(1)}) fusion(s32[3,8,48]{2,1,0:T(8,128)} %param.15), kind=kLoop, calls=%fused_computation.30 | loop fusion | bytes 10752 | tf_op jit(solution)/shard_map/slice | solution.py:419
  1.6 0.1 slice_bitcast_fusion.3
  1.7 0.1 broadcast_in_dim.115
  1.8 0.1 broadcast_in_dim.116
  1.9 1.0 %convert_reduce_fusion = s32[8,48]{1,0:T(8,128)S(1)} fusion(s32[8,48]{1,0:T(8,128)S(1)} %get-tuple-element.14, pred[48,48]{1,0:T(8,128)(4,1)} %constant.65), kind=kLoop, calls=%fused_computation.1 | loop fusion | flops 73344 | bytes 5376 | tf_op jit(solution)/shard_map/reduce_sum | solution.py:422
  2.9 0.1 add_add_fusion
  3.0 0.9 %select_reduce_fusion = s32[48]{0:T(128)S(1)} fusion(s32[8,48]{1,0:T(8,128)S(1)} %add_add_fusion, s32[8,48]{1,0:T(8,128)S(1)} %get-tuple-element.16, pred[8,48]{1,0:T(8,128)(4,1)S(1)} %compare_bitcast_fusion), kind=kLoop, calls=%fused_computation | loop fusion | flops 73680 | bytes 3648 | tf_op jit(solution)/shard_map/reduce_sum | solution.py:425
  3.9 0.1 broadcast_in_dim.118
  4.0 0.1 broadcast_in_dim.119
  4.1 0.1 broadcast_in_dim.113
  4.2 0.1 reshape.242.ymask_ref
  4.3 0.1 add_select_fusion
  4.3 0.1 select_n.71
  4.5 0.1 add_select_fusion.1
  4.5 0.1 select_n.67.target_ref
  4.6 0.1 broadcast_select_fusion.zmask_ref
  4.7 0.1 copy.15.zsrc_ref
  4.8 15.0 %exchange.1 = (bf16[8,48,320]{2,1,0:T(8,128)(2,1)S(1)}, f32[5,4,64,128]{3,2,1,0:T(8,128)S(1)}, bf16[5,64,256]{2,1,0:T(8,128)(2,1)S(1)}, bf16[5,64,128]{2,1,0:T(8,128)(2,1)S(1)}) custom-call(s32[1,384]{1,0:T(1,128)S(1)} %select_n.67.target_ref, bf16[5,64,64,128]{3,2,1,0:T(8,128)(2,1)} %bitcast.38), custom_call_target="tpu_custom_call" | custom-call | tf_op jit(solution)/shard_map/exchange/pallas_call | solution.py:446
  19.9 0.0 copy-done.4
  19.9 0.0 copy-done.2
  19.9 0.0 copy-done.3
  19.9 0.0 copy-done.1
  19.9 0.0 copy-done
  19.9 20.1 %flux_and_penalty.1 = bf16[5,64,64,128]{3,2,1,0:T(8,128)(2,1)} custom-call(f32[64]{0:T(128)S(1)} %copy-done.4, bf16[5,64,64,128]{3,2,1,0:T(8,128)(2,1)} %bitcast.39, f32[5,4,64,128]{3,2,1,0:T(8,128)S(1)} %get-tuple-element.9.edge_ref, bf16[384,320]{1,0:T(8,128)(2,1)S(1)} %bitcast.37, s32[1,256]{1,0:T(1,128)S(1)} %slice.59.ysrc_ref, ...), custom_call_target="tpu_custom_call" | custom-call | tf_op jit(solution)/shard_map/flux_and_penalty/pallas_call | solution.py:494
  (11 shorter events, 0.1 us)
Async XLA Ops:
  0.0 19.9 %copy-start.4 = (f32[64]{0:T(128)S(1)}, f32[64]{0:T(128)}, u32[]{:S(2)}) copy-start(f32[64]{0:T(128)} %constant.59.clone.upper_ref) | copy-start | bytes 772
  0.0 19.9 %copy-start.2 = (bf16[256,128]{1,0:T(8,128)(2,1)S(1)}, bf16[256,128]{1,0:T(8,128)(2,1)}, u32[]{:S(2)}) copy-start(bf16[256,128]{1,0:T(8,128)(2,1)} %constant.58.clone.dz_ref) | copy-start | bytes 196612
  0.0 19.9 %copy-start.3 = (bf16[64,128]{1,0:T(8,128)(2,1)S(1)}, bf16[64,128]{1,0:T(8,128)(2,1)}, u32[]{:S(2)}) copy-start(bf16[64,128]{1,0:T(8,128)(2,1)} %constant.57.clone.dy_ref) | copy-start | bytes 49156
  0.0 19.9 %copy-start.1 = (bf16[1,64,64,128]{3,2,1,0:T(8,128)(2,1)S(1)}, bf16[1,64,64,128]{3,2,1,0:T(8,128)(2,1)}, u32[]{:S(2)}) copy-start(bf16[1,64,64,128]{3,2,1,0:T(8,128)(2,1)} %param.13) | copy-start | bytes 3145732
  0.0 19.9 %copy-start = (bf16[1,64,64,128]{3,2,1,0:T(8,128)(2,1)S(1)}, bf16[1,64,64,128]{3,2,1,0:T(8,128)(2,1)}, u32[]{:S(2)}) copy-start(bf16[1,64,64,128]{3,2,1,0:T(8,128)(2,1)} %param.11) | copy-start | bytes 3145732

commit v4 on v3

--- a/solution.py
+++ b/solution.py
@@ -46,7 +46,7 @@
 
 def exchange_kernel(
     nx, ny, nz, blocks, segments, inverse, end_rows,
-    target_ref, adj_ref, recv_ref, edge_ref, yown_ref, zown_ref,
+    links_ref, adj_ref, edge_ref, ypen_ref, zpen_ref,
     fields, send_ref, yface, zface,
     landed, halo, ends, outgoing, beside,
     load_sem, patch_send, patch_recv, line_send, line_recv,
@@ -111,6 +111,58 @@
     def _():
         halo[1] = jnp.zeros_like(halo[1])
         beside[1] = jnp.zeros_like(beside[1])
+
+    capacity = send_ref.shape[1] // PW
+    source, face, turn = links_ref[0], links_ref[1], links_ref[2]
+    patch_count = source.shape[1]
+    number = lax.broadcasted_iota(jnp.int32, source.shape, 1)
+    owner = lax.broadcasted_iota(jnp.int32, source.shape, 0)
+    slot = jnp.zeros(source.shape, jnp.int32)
+    for k in range(patch_count):
+        slot = slot + jnp.where((source == source[:, k : k + 1]) & (number > k), 1, 0)
+    taken = jnp.where(source == me, owner * capacity + slot + 1, 0)
+    slot_of = jnp.zeros(source.shape, jnp.int32)
+    for k in range(patch_count):
+        slot_of = slot_of + jnp.where(face[:, k : k + 1] == number, taken[:, k : k + 1], 0)
+    slot_of = jnp.sum(slot_of.astype(f32), axis=0, keepdims=True) - 1.0
+
+    def own(values):
+        return jnp.sum(jnp.where(owner == me, values, 0).astype(f32), axis=0, keepdims=True)
+
+    own_source = own(source)
+    origin_slot = jnp.where(own_source >= 0.0, own_source * capacity + own(slot), -1.0)
+    live = jnp.where(own_source >= 0.0, penalty_weight, 0.0)
+    facts = jnp.concatenate([slot_of, origin_slot, own(turn), live] * 2, axis=0).astype(bf16)
+    cells_all = 2 * nz + 2 * ny
+    spread = jnp.where(
+        lax.broadcasted_iota(jnp.int32, (patch_count, cells_all), 0)
+        == lax.broadcasted_iota(jnp.int32, (patch_count, cells_all), 1) // PW,
+        1.0,
+        0.0,
+    ).astype(bf16)
+    by_lane = jnp.dot(facts, spread, preferred_element_type=f32)
+    spread_z = jnp.where(
+        lax.broadcasted_iota(jnp.int32, (2 * ny, patch_count), 0) // PW + 2 * nz // PW
+        == lax.broadcasted_iota(jnp.int32, (2 * ny, patch_count), 1),
+        1.0,
+        0.0,
+    ).astype(bf16)
+    by_row = lax.dot_general(
+        spread_z, facts, (((1,), (1,)), ((), ())), preferred_element_type=f32
+    )
+    cell = (lax.broadcasted_iota(jnp.int32, (1, cells_all), 1) % PW).astype(f32)
+    cell_z = (lax.broadcasted_iota(jnp.int32, (2 * ny, 1), 0) % PW).astype(f32)
+
+    def spot_of(slots, turned, cells):
+        return jnp.where(
+            slots >= 0.0, slots * PW + jnp.where(turned > 0.5, PW - 1.0 - cells, cells), -1.0
+        )
+
+    target = spot_of(by_lane[0:1], jnp.zeros_like(cell), cell)
+    yorigin = spot_of(by_lane[1:2], by_lane[2:3], cell)[:, : 2 * nz]
+    zorigin = spot_of(by_row[:, 1:2], by_row[:, 2:3], cell_z)
+    ylive = by_lane[3:4, : 2 * nz]
+    zlive = by_row[:, 3:4]
 
     pl.semaphore_wait(
         barrier, blocks - 1 + has_left.astype(jnp.int32) + has_right.astype(jnp.int32)
@@ -198,7 +250,7 @@
     own_rows = yface[...].astype(bf16)
     rows = blocks * send_ref.shape[1]
     slots = lax.broadcasted_iota(jnp.int32, (rows, 2 * nz + 2 * ny), 0)
-    chosen = jnp.where(slots == target_ref[...], 1.0, 0.0).astype(bf16)
+    chosen = jnp.where(slots.astype(f32) == target, 1.0, 0.0).astype(bf16)
     packed = lax.dot_general(
         chosen[:, : 2 * nz],
         own_rows.reshape(FIELDS * nx, 2 * nz),
@@ -211,9 +263,7 @@
     patches = [patch_copy(shift) for shift in range(1, blocks)]
     for copy in patches:
         copy.start()
-    recv_ref[me] = send_ref[me]
-    yown_ref[...] = own_rows
-    zown_ref[...] = zface[...]
+    landed[me] = send_ref[me]
 
     corner_first = float(inverse[0, 0])
     corner_last = float(inverse[nx - 1, nx - 1])
@@ -239,10 +289,29 @@
         edge_ref[f, 2] = terms[2]
         edge_ref[f, 3] = terms[3] - jnp.where(has_right, lhs_alpha * right, 0.0)
 
-    for shift, copy in enumerate(patches, 1):
+    for copy in patches:
         copy.wait_recv()
-        origin = lax.rem(me + blocks - shift, blocks)
-        recv_ref[origin] = landed[origin]
+    received = landed[...].reshape(rows, FIELDS * nx)
+    slots = lax.broadcasted_iota(jnp.int32, (rows, 2 * nz), 0)
+    ypick = jnp.where(slots.astype(f32) == yorigin, 1.0, 0.0).astype(bf16)
+    yother = lax.dot_general(
+        received, ypick, (((0,), (0,)), ((), ())), preferred_element_type=f32
+    ).reshape(FIELDS, nx, 2 * nz)
+    ypen_ref[...] = ylive * (yother - yface[...])
+    slots = lax.broadcasted_iota(jnp.int32, (2 * ny, rows), 1)
+    zpick = jnp.where(slots.astype(f32) == zorigin, 1.0, 0.0).astype(bf16)
+    zcells = jnp.dot(zpick, received, preferred_element_type=f32).astype(bf16)
+    row = lax.broadcasted_iota(jnp.int32, (2 * nx, nz), 0)
+    col = lax.broadcasted_iota(jnp.int32, (2 * nx, nz), 1)
+    wanted = jnp.where(row < nx, 2 * row + 1, 2 * (row - nx))
+    order = jnp.where(col == wanted, 1.0, 0.0).astype(bf16)
+    zmask = jnp.where(lane % 2 == 1, zlive[:ny], zlive[ny:])
+    for f in range(FIELDS):
+        both = jnp.concatenate(
+            [zcells[:ny, f * nx : (f + 1) * nx], zcells[ny:, f * nx : (f + 1) * nx]], axis=1
+        )
+        zother = jnp.dot(both, order, preferred_element_type=f32)
+        zpen_ref[f] = zmask * (zother - zface[f].astype(f32))
     for copy in patches:
         copy.wait_send()
 
@@ -259,11 +328,10 @@
 
 def main_kernel(
     nx, ny, nz, bx,
-    upper_ref, adj_hbm, edge_ref, recv_ref, ysrc_ref, zsrc_ref, ymask_ref, zmask_ref,
-    yown_ref, zown_ref,
+    upper_ref, adj_hbm, edge_ref, ypen, zpen,
     dy_ref, dz_ref, rho_ref, vel_ref, prs_ref, met_ref,
     out_ref,
-    adj_ref, load_sem, sweep, ypen, zpen, carry, gyz,
+    adj_ref, load_sem, sweep, carry, gyz,
 ):
     step = pl.program_id(0)
     block = pl.num_programs(0) - 1 - step
@@ -283,28 +351,6 @@
         for f in range(FIELDS):
             for h in range(2):
                 load(f, h).start()
-        rows = recv_ref.shape[0]
-        received = recv_ref[...]
-        slots = lax.broadcasted_iota(jnp.int32, (rows, 2 * nz), 0)
-        ypick = jnp.where(slots == ysrc_ref[...], 1.0, 0.0).astype(bf16)
-        yother = lax.dot_general(
-            received, ypick, (((0,), (0,)), ((), ())), preferred_element_type=f32
-        ).reshape(FIELDS, nx, 2 * nz)
-        ypen[...] = ymask_ref[...] * (yother - yown_ref[...].astype(f32))
-        slots = lax.broadcasted_iota(jnp.int32, (2 * ny, rows), 1)
-        zpick = jnp.where(slots == zsrc_ref[...], 1.0, 0.0).astype(bf16)
-        zcells = jnp.dot(zpick, received, preferred_element_type=f32).astype(bf16)
-        row = lax.broadcasted_iota(jnp.int32, (2 * nx, nz), 0)
-        col = lax.broadcasted_iota(jnp.int32, (2 * nx, nz), 1)
-        wanted = jnp.where(row < nx, 2 * row + 1, 2 * (row - nx))
-        order = jnp.where(col == wanted, 1.0, 0.0).astype(bf16)
-        for f in range(FIELDS):
-            both = jnp.concatenate(
-                [zcells[:ny, f * nx : (f + 1) * nx], zcells[ny:, f * nx : (f + 1) * nx]], axis=1
-            )
-            zother = jnp.dot(both, order, preferred_element_type=f32)
-            zpen[f] = zmask_ref[...] * (zother - zown_ref[f].astype(f32))
-
         def forward(index, state):
             f = index // (ny // part)
             at = pl.ds(pl.multiple_of((index % (ny // part)) * part, part), part)
@@ -320,12 +366,13 @@
             for x in range(nx):
                 ahead = adj_ref[f, x + 2, at, :].astype(f32) if x + 2 < nx else zero
                 window.append(ahead)
-                total = near_coef * (window[3] - window[1]) + far_coef * (window[4] - window[0])
-                if x < 2:
-                    total = total + edge_ref[f, x, at, :]
-                elif x >= nx - 2:
-                    total = total + edge_ref[f, x - nx + 4, at, :]
-                before = float(weight[x]) * total - float(upper[x]) * before
+                total = near_coef / far_coef * (window[3] - window[1]) + (window[4] - window[0])
+                scale = float(weight[x])
+                if x < 2 or x >= nx - 2:
+                    total = far_coef * total + edge_ref[f, x if x < 2 else x - nx + 4, at, :]
+                else:
+                    scale = scale * far_coef
+                before = scale * total - float(upper[x]) * before
                 sweep[f, x, at, :] = before
                 window = window[1:]
             return state
@@ -334,7 +381,7 @@
         carry[...] = jnp.zeros_like(carry)
 
     chunk = 16 if ny % 16 == 0 else ny
-    unroll = 2
+    unroll = 4
     row = lax.broadcasted_iota(jnp.int32, (chunk, nz), 0)
     lane = lax.broadcasted_iota(jnp.int32, (chunk, nz), 1)
     zedge = (lane == 0) | (lane == nz - 1)
@@ -412,49 +459,24 @@
     blocks, patches = links.shape[1:]
     blk_count = lax.axis_size("blk")
     segments = lax.axis_size("ax")
-    me = lax.axis_index("blk")
     capacity = -(-patches // blocks)
     inverse, derivative = tables(nx)
 
-    source, face, turn = links[0], links[1], links[2]
-    earlier = np.tril(np.ones((patches, patches), bool), -1)[None]
-    same = (source[:, :, None] == source[:, None, :]) & earlier
-    slot = jnp.sum(same.astype(jnp.int32), axis=2)
-    place = jnp.arange(blocks, dtype=jnp.int32)[:, None] * capacity + slot
-    mine = (source == me)[None] & (face[None] == jnp.arange(patches, dtype=jnp.int32)[:, None, None])
-    slot_of = jnp.sum(jnp.where(mine, place[None] + 1, 0), axis=(1, 2)) - 1
-    cell = jnp.arange(PW, dtype=jnp.int32)[None, :]
-    target = jnp.where(slot_of[:, None] >= 0, slot_of[:, None] * PW + cell, -1).reshape(1, -1)
-    own_source = lax.dynamic_index_in_dim(source, me, 0, keepdims=False)[:, None]
-    own_slot = lax.dynamic_index_in_dim(slot, me, 0, keepdims=False)[:, None]
-    own_turn = lax.dynamic_index_in_dim(turn, me, 0, keepdims=False)[:, None]
-    origin = (own_source * capacity + own_slot) * PW + jnp.where(own_turn == 1, PW - 1 - cell, cell)
-    origin = jnp.where(own_source >= 0, origin, -1).reshape(1, -1)
-    live = penalty_weight * jnp.broadcast_to(
-        (own_source >= 0).astype(f32), (patches, PW)
-    ).reshape(-1)
-    ymask = live[: 2 * nz].reshape(1, 2 * nz)
-    zlive = live[2 * nz :].reshape(2, ny)
-    column = jnp.arange(nz, dtype=jnp.int32)[None, :]
-    zmask = jnp.where(column % 2 == 1, zlive[0][:, None], zlive[1][:, None])
-
-    rows = blk_count * capacity * PW
     slab = (capacity * PW, FIELDS * nx)
     layers = (FIELDS, 2, ny, nz)
     level = (FIELDS, ny, nz)
     vmem = pl.BlockSpec(memory_space=pltpu.VMEM)
-    recv, edges, yown, zown = pl.pallas_call(
+    edges, ypen, zpen = pl.pallas_call(
         functools.partial(
             exchange_kernel, nx, ny, nz, blk_count, segments, inverse, derivative[[0, nx - 1]]
         ),
         out_shape=(
-            jax.ShapeDtypeStruct((blk_count,) + slab, bf16),
             jax.ShapeDtypeStruct((FIELDS, 4, ny, nz), f32),
-            jax.ShapeDtypeStruct((FIELDS, nx, 2 * nz), bf16),
-            jax.ShapeDtypeStruct((FIELDS, ny, nz), bf16),
+            jax.ShapeDtypeStruct((FIELDS, nx, 2 * nz), f32),
+            jax.ShapeDtypeStruct((FIELDS, ny, nz), f32),
         ),
         in_specs=[vmem, pl.BlockSpec(memory_space=pl.ANY)],
-        out_specs=(vmem, vmem, vmem, vmem),
+        out_specs=(vmem, vmem, vmem),
         scratch_shapes=[
             pltpu.VMEM((FIELDS, nx, ny, nz), bf16),
             pltpu.VMEM((blk_count,) + slab, bf16),
@@ -475,8 +497,7 @@
             collective_id=0, has_side_effects=True, vmem_limit_bytes=48 << 20
         ),
         name="exchange",
-    )(target, adj)
-    recv = recv.reshape(rows, FIELDS * nx)
+    )(links, adj)
 
     dy_high, dy_low = split(tables(ny)[1])
     dz_high, dz_low = split(tables(nz)[1])
@@ -499,11 +520,6 @@
             pl.BlockSpec(memory_space=pltpu.SMEM),
             pl.BlockSpec(memory_space=pl.ANY),
             whole(FIELDS, 4, ny, nz),
-            whole(rows, FIELDS * nx),
-            whole(1, 2 * nz),
-            whole(2 * ny, 1),
-            whole(1, 2 * nz),
-            whole(ny, nz),
             whole(FIELDS, nx, 2 * nz),
             whole(FIELDS, ny, nz),
             whole(ny, 2 * ny),
@@ -518,17 +534,14 @@
             pltpu.VMEM((FIELDS, nx, ny, nz), bf16),
             pltpu.SemaphoreType.DMA((2 * FIELDS,)),
             pltpu.VMEM((FIELDS, nx, ny, nz), f32),
-            pltpu.VMEM((FIELDS, nx, 2 * nz), f32),
             pltpu.VMEM((FIELDS, ny, nz), f32),
-            pltpu.VMEM((FIELDS, ny, nz), f32),
-            pltpu.VMEM((2, 2, FIELDS, ny, nz), f32),
+            pltpu.VMEM((4, 2, FIELDS, ny, nz), f32),
         ],
         compiler_params=pltpu.CompilerParams(vmem_limit_bytes=48 << 20),
         name="flux_and_penalty",
     )(
-        upper, adj, edges, recv,
-        origin[:, : 2 * nz], origin[:, 2 * nz :].reshape(2 * ny, 1), ymask, zmask,
-        yown, zown, dy_both, dz_both, density[0], velocity[:, 0], pressure[0], metrics[:, 0],
+        upper, adj, edges, ypen, zpen, dy_both, dz_both,
+        density[0], velocity[:, 0], pressure[0], metrics[:, 0],
     )
     return result[:, None]
 

time: 40.3 us -> 36.4 us (0.903)
  other arithmetic: 3.17 us -> 0 us
  local copies, waits for them, and re-layouts: 1.59 us -> 0.87 us
    reduce_sum x2 -> x0, other arithmetic: 1.95 us -> none  [the longest x1 1 us: body(): slot = jnp.sum(same.astype(jnp.int32), axis=2)]
    unnamed x10 -> x12, local copies, waits for them, and re-layouts: 0.02 us -> 0.87 us
    and x1 -> x0, other arithmetic: 0.84 us -> none  [body(): (source == me)[None]]
    slice x4 -> x0, local copies, waits for them, and re-layouts: 0.8 us -> none  [the longest x1 0.72 us: body(): source, face, turn = (links[0], links[1], links[2])]
    pallas_call x1, Pallas kernels: 15 us -> 15.5 us  [body(): pl.pallas_call(functools.partial(exchange_kernel, nx, ny, nz, blk_count,...]
where the time goes in v4:
time: 36.4 us; the launch traced here: 36.1 us
  Pallas kernels  35.2 us (97%)
  local copies, waits for them, and re-layouts  0.87 us (2%)
    pallas_call x1, Pallas kernels, body(): pl.pallas_call(functools.partial(main_kernel, nx, ny, nz, bx), grid=(step...  19.7 us
    pallas_call x1, Pallas kernels, body(): pl.pallas_call(functools.partial(exchange_kernel, nx, ny, nz, blk_count,...  15.5 us
    unnamed x12, local copies, waits for them, and re-layouts  0.87 us

profile of v4, /device:TPU:0, one launch (start us, length us, event | category | flops | bytes accessed | tf_op | source)
XLA Modules:
  0.0 36.1 jit_solution(13685798943929265040)
XLA Ops:
  0.0 0.0 copy-start.5
  0.0 0.0 copy-start.2
  0.0 0.0 copy-start.3
  0.0 0.0 copy-start.1
  0.0 0.0 copy-start
  0.0 0.0 copy-start.4
  0.0 0.8 %copy-done.4 = s32[3,8,48]{2,1,0:T(8,128)S(1)} copy-done((s32[3,8,48]{2,1,0:T(8,128)S(1)}, s32[3,8,48]{2,1,0:T(8,128)}, u32[]{:S(2)}) %copy-start.4) | copy-done | bytes 4632
  0.9 15.5 %exchange.1 = (f32[5,4,64,128]{3,2,1,0:T(8,128)S(1)}, f32[5,64,256]{2,1,0:T(8,128)S(1)}, f32[5,64,128]{2,1,0:T(8,128)S(1)}) custom-call(s32[3,8,48]{2,1,0:T(8,128)S(1)} %copy-done.4, bf16[5,64,64,128]{3,2,1,0:T(8,128)(2,1)} %bitcast.10), custom_call_target="tpu_custom_call" | custom-call | tf_op jit(solution)/shard_map/exchange/pallas_call | solution.py:469
  16.4 0.0 copy-done.5
  16.4 0.0 copy-done.2
  16.4 0.0 copy-done.3
  16.4 0.0 copy-done.1
  16.4 0.0 copy-done
  16.4 19.7 %flux_and_penalty.1 = bf16[5,64,64,128]{3,2,1,0:T(8,128)(2,1)} custom-call(f32[64]{0:T(128)S(1)} %copy-done.5, bf16[5,64,64,128]{3,2,1,0:T(8,128)(2,1)} %bitcast.11, f32[5,4,64,128]{3,2,1,0:T(8,128)S(1)} %get-tuple-element.8.edge_ref, f32[5,64,256]{2,1,0:T(8,128)S(1)} %get-tuple-element.9.ypen, f32[5,64,128]{2,1,0:T(8,128)S(1)} %get-tuple-element.10.zpen, ...), custom_call_target="tpu_custom_call" | custom-call | tf_op jit(solution)/shard_map/flux_and_penalty/pallas_call | solution.py:515
Async XLA Ops:
  0.0 16.4 %copy-start.5 = (f32[64]{0:T(128)S(1)}, f32[64]{0:T(128)}, u32[]{:S(2)}) copy-start(f32[64]{0:T(128)} %constant.8.clone.upper_ref) | copy-start | bytes 772
  0.0 16.4 %copy-start.2 = (bf16[256,128]{1,0:T(8,128)(2,1)S(1)}, bf16[256,128]{1,0:T(8,128)(2,1)}, u32[]{:S(2)}) copy-start(bf16[256,128]{1,0:T(8,128)(2,1)} %constant.7.clone.dz_ref) | copy-start | bytes 196612
  0.0 16.4 %copy-start.3 = (bf16[64,128]{1,0:T(8,128)(2,1)S(1)}, bf16[64,128]{1,0:T(8,128)(2,1)}, u32[]{:S(2)}) copy-start(bf16[64,128]{1,0:T(8,128)(2,1)} %constant.6.clone.dy_ref) | copy-start | bytes 49156
  0.0 16.4 %copy-start.1 = (bf16[1,64,64,128]{3,2,1,0:T(8,128)(2,1)S(1)}, bf16[1,64,64,128]{3,2,1,0:T(8,128)(2,1)}, u32[]{:S(2)}) copy-start(bf16[1,64,64,128]{3,2,1,0:T(8,128)(2,1)} %param.12) | copy-start | bytes 3145732
  0.0 16.4 %copy-start = (bf16[1,64,64,128]{3,2,1,0:T(8,128)(2,1)S(1)}, bf16[1,64,64,128]{3,2,1,0:T(8,128)(2,1)}, u32[]{:S(2)}) copy-start(bf16[1,64,64,128]{3,2,1,0:T(8,128)(2,1)} %param.10) | copy-start | bytes 3145732
  0.0 0.9 %copy-start.4 = (s32[3,8,48]{2,1,0:T(8,128)S(1)}, s32[3,8,48]{2,1,0:T(8,128)}, u32[]{:S(2)}) copy-start(s32[3,8,48]{2,1,0:T(8,128)} %links_ref.1) | copy-start | bytes 13828

commit v5 on v4

--- a/solution.py
+++ b/solution.py
@@ -329,10 +329,11 @@
 def main_kernel(
     nx, ny, nz, bx,
     upper_ref, adj_hbm, edge_ref, ypen, zpen,
-    dy_ref, dz_ref, rho_ref, vel_ref, prs_ref, met_ref,
+    dy_ref, dz_ref, rho_ref, vel_ref, prs_ref, met_x_ref, met_y_ref, met_z_ref,
     out_ref,
     adj_ref, load_sem, sweep, carry, gyz,
 ):
+    metric_refs = (met_x_ref, met_y_ref, met_z_ref)
     step = pl.program_id(0)
     block = pl.num_programs(0) - 1 - step
     weight, upper = sweep_coefs(nx)
@@ -420,7 +421,7 @@
 
             turned = None
             for d, g in enumerate((gx, gy, gz)):
-                k = [met_ref[3 * d + c, j, at, :].astype(f32) for c in range(3)]
+                k = [metric_refs[d][c, j, at, :].astype(f32) for c in range(3)]
                 speed = k[0] * vel[0] + k[1] * vel[1] + k[2] * vel[2]
                 coupled = rho * g[0] + prs * g[4]
                 for i in range(FIELDS):
@@ -512,6 +513,9 @@
         zeros = (0,) * len(shape)
         return pl.BlockSpec(shape, lambda i: zeros, pipeline_mode=pl.Buffered(1))
 
+    def metric(d):
+        return pl.BlockSpec((3, bx, ny, nz), lambda i: (d, steps - 1 - i, 0, 0))
+
     result = pl.pallas_call(
         functools.partial(main_kernel, nx, ny, nz, bx),
         grid=(steps,),
@@ -527,7 +531,9 @@
             pl.BlockSpec((bx, ny, nz), lambda i: (steps - 1 - i, 0, 0)),
             pl.BlockSpec((3, bx, ny, nz), lambda i: (0, steps - 1 - i, 0, 0)),
             pl.BlockSpec((bx, ny, nz), lambda i: (steps - 1 - i, 0, 0)),
-            pl.BlockSpec((9, bx, ny, nz), lambda i: (0, steps - 1 - i, 0, 0)),
+            metric(0),
+            metric(1),
+            metric(2),
         ],
         out_specs=pl.BlockSpec((FIELDS, bx, ny, nz), lambda i: (0, steps - 1 - i, 0, 0)),
         scratch_shapes=[
@@ -541,7 +547,8 @@
         name="flux_and_penalty",
     )(
         upper, adj, edges, ypen, zpen, dy_both, dz_both,
-        density[0], velocity[:, 0], pressure[0], metrics[:, 0],
+        density[0], velocity[:, 0], pressure[0],
+        metrics[:, 0], metrics[:, 0], metrics[:, 0],
     )
     return result[:, None]
 

time: 36.4 us -> 36.3 us (level)
  no operation moved by 1% of the time
where the time goes in v5:
time: 36.3 us; the launch traced here: 36.1 us
  Pallas kernels  35.2 us (97%)
  local copies, waits for them, and re-layouts  0.87 us (2%)
    pallas_call x1, Pallas kernels, body(): pl.pallas_call(functools.partial(main_kernel, nx, ny, nz, bx), grid=(step...  19.7 us
    pallas_call x1, Pallas kernels, body(): pl.pallas_call(functools.partial(exchange_kernel, nx, ny, nz, blk_count,...  15.5 us
    unnamed x12, local copies, waits for them, and re-layouts  0.87 us

profile of v5, /device:TPU:0, one launch (start us, length us, event | category | flops | bytes accessed | tf_op | source)
XLA Modules:
  0.0 36.1 jit_solution(17070491608601015081)
XLA Ops:
  0.0 0.0 copy-start.5
  0.0 0.0 copy-start.2
  0.0 0.0 copy-start.3
  0.0 0.0 copy-start.1
  0.0 0.0 copy-start
  0.0 0.0 copy-start.4
  0.0 0.8 %copy-done.4 = s32[3,8,48]{2,1,0:T(8,128)S(1)} copy-done((s32[3,8,48]{2,1,0:T(8,128)S(1)}, s32[3,8,48]{2,1,0:T(8,128)}, u32[]{:S(2)}) %copy-start.4) | copy-done | bytes 4632
  0.9 15.5 %exchange.1 = (f32[5,4,64,128]{3,2,1,0:T(8,128)S(1)}, f32[5,64,256]{2,1,0:T(8,128)S(1)}, f32[5,64,128]{2,1,0:T(8,128)S(1)}) custom-call(s32[3,8,48]{2,1,0:T(8,128)S(1)} %copy-done.4, bf16[5,64,64,128]{3,2,1,0:T(8,128)(2,1)} %bitcast.13), custom_call_target="tpu_custom_call" | custom-call | tf_op jit(solution)/shard_map/exchange/pallas_call | solution.py:470
  16.4 0.0 copy-done.5
  16.4 0.0 copy-done.2
  16.4 0.0 copy-done.3
  16.4 0.0 copy-done.1
  16.4 0.0 copy-done
  16.4 19.7 %flux_and_penalty.1 = bf16[5,64,64,128]{3,2,1,0:T(8,128)(2,1)} custom-call(f32[64]{0:T(128)S(1)} %copy-done.5, bf16[5,64,64,128]{3,2,1,0:T(8,128)(2,1)} %bitcast.14, f32[5,4,64,128]{3,2,1,0:T(8,128)S(1)} %get-tuple-element.8.edge_ref, f32[5,64,256]{2,1,0:T(8,128)S(1)} %get-tuple-element.9.ypen, f32[5,64,128]{2,1,0:T(8,128)S(1)} %get-tuple-element.10.zpen, ...), custom_call_target="tpu_custom_call" | custom-call | tf_op jit(solution)/shard_map/flux_and_penalty/pallas_call | solution.py:519
Async XLA Ops:
  0.0 16.4 %copy-start.5 = (f32[64]{0:T(128)S(1)}, f32[64]{0:T(128)}, u32[]{:S(2)}) copy-start(f32[64]{0:T(128)} %constant.8.clone.upper_ref) | copy-start | bytes 772
  0.0 16.4 %copy-start.2 = (bf16[256,128]{1,0:T(8,128)(2,1)S(1)}, bf16[256,128]{1,0:T(8,128)(2,1)}, u32[]{:S(2)}) copy-start(bf16[256,128]{1,0:T(8,128)(2,1)} %constant.7.clone.dz_ref) | copy-start | bytes 196612
  0.0 16.4 %copy-start.3 = (bf16[64,128]{1,0:T(8,128)(2,1)S(1)}, bf16[64,128]{1,0:T(8,128)(2,1)}, u32[]{:S(2)}) copy-start(bf16[64,128]{1,0:T(8,128)(2,1)} %constant.6.clone.dy_ref) | copy-start | bytes 49156
  0.0 16.4 %copy-start.1 = (bf16[1,64,64,128]{3,2,1,0:T(8,128)(2,1)S(1)}, bf16[1,64,64,128]{3,2,1,0:T(8,128)(2,1)}, u32[]{:S(2)}) copy-start(bf16[1,64,64,128]{3,2,1,0:T(8,128)(2,1)} %param.12) | copy-start | bytes 3145732
  0.0 16.4 %copy-start = (bf16[1,64,64,128]{3,2,1,0:T(8,128)(2,1)S(1)}, bf16[1,64,64,128]{3,2,1,0:T(8,128)(2,1)}, u32[]{:S(2)}) copy-start(bf16[1,64,64,128]{3,2,1,0:T(8,128)(2,1)} %param.10) | copy-start | bytes 3145732
  0.0 0.9 %copy-start.4 = (s32[3,8,48]{2,1,0:T(8,128)S(1)}, s32[3,8,48]{2,1,0:T(8,128)}, u32[]{:S(2)}) copy-start(s32[3,8,48]{2,1,0:T(8,128)} %links_ref.1) | copy-start | bytes 13828
